TPU v7x, 32 devices: a whole 2x2x4 slice. The times are simulated.
32 devices in a mesh: ctx: 8 (over z, x), tensor: 2 (over core), dp: 2 (over y).
Axes of the slice: x: 2, y: 2, z: 4, core: 2. Of those that a mesh axis runs over, the one named last changes fastest.
Arguments:
- cache: bfloat16 [8, 8, 4096, 256], P('dp', 'tensor', 'ctx'), may hold values from -6 to 6
- kept: int32 [8, 8, 1024], P('dp', 'tensor'), may hold values from 0 to 4095, as said below
- assign: int32 [8], replicated, may hold values from 0 to 7, each once
- queries: bfloat16 [8, 128, 8192], P('ctx', 'dp', 'tensor'), may hold values from -140 to 140
- new_kv: bfloat16 [8, 128, 8, 256], P('ctx', 'dp', 'tensor'), may hold values from -5 to 5
- out_weight: bfloat16 [8192, 8192], P('tensor', 'ctx'), may hold values from -0.0625 to 0.0625
Outputs:
- output: bfloat16 [8, 128, 8192], P('tensor', 'dp', 'ctx')
Inputs may be any that keep to these rules, and one draw needn't show every extreme that they name: Each kept[p, t] lists 1024 distinct positions in increasing order; block b holds positions b * 512 to (b + 1) * 512 - 1; at most 256 positions of one list fall in one block, and in every list some block holds exactly 256. `assign`: every slot 0 to 7 is given to exactly one prompt.
All inputs are finite; a program needn't handle non-finite values.
Results may differ from a plain program's by a relative error of at most 0.029.
Values may be sent and summed in bfloat16 or wider, within the bound.
A program may use at most 64 MiB of HBM per device.

v0:
```python
import jax
import jax.numpy as jnp
from jax import lax
from jax.sharding import PartitionSpec as P

neg_large = -1e30


def swapped(array, axis, distance):
    return lax.ppermute(array, axis, [(i, i ^ 1 << distance) for i in range(lax.axis_size(axis))])


def slot_prompt(assign, slot_id):
    matches = (assign == slot_id).astype(jnp.int32)
    return jnp.sum(matches * jnp.arange(assign.shape[0], dtype=jnp.int32))


def block_rows_of(flat_cache, kept_lists, block_start, first_rank, row_count, stride, capacity):
    offsets = jnp.arange(capacity, dtype=jnp.int32)
    rank_ids = jnp.clip(first_rank[:, None] + stride * offsets[None, :], 0, kept_lists.shape[1] - 1)
    places = jnp.take_along_axis(kept_lists, rank_ids, axis=1) - block_start
    is_valid = offsets[None, :] < row_count[:, None]
    spots = jnp.arange(flat_cache.shape[1], dtype=jnp.int32)
    chooser = ((places[:, :, None] == spots[None, None, :]) & is_valid[:, :, None]).astype(
        flat_cache.dtype
    )
    picked = jnp.einsum("gcq,gqw->gcw", chooser, flat_cache, preferred_element_type=jnp.float32)
    return picked.astype(flat_cache.dtype)


def padded_layout(rows, marks):
    senders, kv_here, capacity, row_width = rows.shape
    flat_rows = jnp.transpose(rows, (1, 0, 2, 3)).reshape(kv_here, senders * capacity, row_width)
    flat_marks = jnp.transpose(marks, (1, 0, 2)).reshape(kv_here, senders * capacity)
    return (flat_rows, flat_marks)


def attend_rows(query, row_start, kept_rows, kept_marks, new_rows, new_start):
    head_dim = kept_rows.shape[2] // 2
    score_scale = head_dim ** (-0.5)
    kept_scores = (
        jnp.einsum(
            "rkgd,knd->rkgn", query, kept_rows[:, :, :head_dim], preferred_element_type=jnp.float32
        )
        * score_scale
    )
    kept_scores = jnp.where((kept_marks > 0.5)[None, :, None, :], kept_scores, neg_large)
    new_scores = (
        jnp.einsum(
            "rkgd,nkd->rkgn", query, new_rows[:, :, :head_dim], preferred_element_type=jnp.float32
        )
        * score_scale
    )
    row_ids = row_start + jnp.arange(query.shape[0], dtype=jnp.int32)
    key_ids = new_start + jnp.arange(new_rows.shape[0], dtype=jnp.int32)
    visible = (key_ids[None, :] <= row_ids[:, None])[:, None, None, :]
    new_scores = jnp.where(visible, new_scores, neg_large)
    row_top = jnp.maximum(jnp.max(kept_scores, axis=3), jnp.max(new_scores, axis=3))
    kept_weights = jnp.exp(kept_scores - row_top[..., None])
    new_weights = jnp.exp(new_scores - row_top[..., None])
    weight_sum = jnp.sum(kept_weights, axis=3) + jnp.sum(new_weights, axis=3)
    weighted = jnp.einsum(
        "rkgn,knd->rkgd",
        kept_weights.astype(jnp.bfloat16),
        kept_rows[:, :, head_dim:],
        preferred_element_type=jnp.float32,
    )
    weighted = weighted + jnp.einsum(
        "rkgn,nkd->rkgd",
        new_weights.astype(jnp.bfloat16),
        new_rows[:, :, head_dim:],
        preferred_element_type=jnp.float32,
    )
    return (row_top, weight_sum, weighted)


def attend(query, row_start, kept_rows, kept_marks, new_rows, new_start):
    half_rows = query.shape[0] // 2
    first = attend_rows(query[:half_rows], row_start, kept_rows, kept_marks, new_rows, new_start)
    second = attend_rows(
        query[half_rows:], row_start + half_rows, kept_rows, kept_marks, new_rows, new_start
    )
    return tuple((jnp.concatenate([first[index], second[index]], axis=0) for index in range(3)))


def local(cache, kept, assign, queries, new_kv, out_weight):
    ctx_count = lax.axis_size("ctx")
    ctx_id = lax.axis_index("ctx")
    dp_id = lax.axis_index("dp")
    groups, kv_here, ctx_dev, row_width = cache.shape
    head_dim = row_width // 2
    keep_total = kept.shape[2]
    flat_cache = cache.reshape(groups * kv_here, ctx_dev, row_width)
    kept_lists = kept.reshape(groups * kv_here, keep_total)
    block_start = ctx_id * ctx_dev
    rank_low = jnp.sum((kept_lists < block_start).astype(jnp.int32), axis=1)
    rank_high = jnp.sum((kept_lists < block_start + ctx_dev).astype(jnp.int32), axis=1)
    slot_ids = lax.dynamic_slice_in_dim(assign, dp_id * groups, groups)
    prompt = slot_prompt(assign, ctx_id)
    capacity = ctx_dev // 2
    row_count = rank_high - rank_low
    picked = block_rows_of(flat_cache, kept_lists, block_start, rank_low, row_count, 1, capacity)
    picked = picked.reshape(groups, kv_here, capacity, row_width)
    buffer = (
        jnp.zeros((ctx_count, kv_here, capacity, row_width), cache.dtype).at[slot_ids].set(picked)
    )
    counts = (
        jnp.zeros((ctx_count, kv_here), jnp.int32)
        .at[slot_ids]
        .set(row_count.reshape(groups, kv_here))
    )
    received, got_counts = (
        lax.all_to_all(buffer, "ctx", split_axis=0, concat_axis=0, tiled=True),
        lax.all_to_all(counts, "ctx", split_axis=0, concat_axis=0, tiled=True),
    )
    halves = received.reshape(ctx_count, kv_here, capacity // 2, 2, row_width)
    offsets = jnp.arange(capacity // 2, dtype=jnp.int32)
    even_marks = (2 * offsets[None, None, :] < got_counts[:, :, None]).astype(cache.dtype)
    odd_marks = (2 * offsets[None, None, :] + 1 < got_counts[:, :, None]).astype(cache.dtype)
    own_rows = jnp.where(dp_id == 0, halves[:, :, :, 0], halves[:, :, :, 1])
    own_marks = jnp.where(dp_id == 0, even_marks, odd_marks)
    their_rows = jnp.where(dp_id == 0, halves[:, :, :, 1], halves[:, :, :, 0])
    their_marks = jnp.where(dp_id == 0, odd_marks, even_marks)
    own_flat, own_flat_marks = padded_layout(own_rows, own_marks)
    their_flat, their_flat_marks = padded_layout(their_rows, their_marks)
    from_partner, partner_marks = swapped((their_flat, their_flat_marks), "dp", 0)
    owner_here = prompt // groups == dp_id
    kept_half = jnp.where(owner_here, own_flat, from_partner)
    kept_marks = jnp.where(owner_here, own_flat_marks, partner_marks)
    rows_here = queries.shape[1]
    per_group = queries.shape[2] // (kv_here * head_dim)
    own_query = queries[0].reshape(rows_here, kv_here, per_group, head_dim)
    own_new = new_kv[0]
    own_start = dp_id * rows_here
    other_kept, other_marks, other_new = swapped((kept_half, kept_marks, own_new), "dp", 0)
    all_kept = jnp.concatenate([kept_half, other_kept], axis=1)
    all_marks = jnp.concatenate([kept_marks, other_marks], axis=1)
    all_new = jnp.where(
        dp_id == 0,
        jnp.concatenate([own_new, other_new], axis=0),
        jnp.concatenate([other_new, own_new], axis=0),
    )
    row_top, weight_sum, weighted = attend(own_query, own_start, all_kept, all_marks, all_new, 0)
    head_out = (
        (weighted / weight_sum[..., None])
        .reshape(rows_here, kv_here * per_group * head_dim)
        .astype(jnp.bfloat16)
    )
    partials = jnp.dot(
        lax.all_gather(head_out, "ctx", axis=0, tiled=True),
        out_weight,
        preferred_element_type=jnp.float32,
    )
    partials = partials.reshape(ctx_count, rows_here, partials.shape[1])[assign]
    return lax.psum_scatter(
        partials.astype(jnp.bfloat16), "tensor", scatter_dimension=0, tiled=True
    )


def solution(mesh):
    placed = (
        P("dp", "tensor", "ctx", None),
        P("dp", "tensor", None),
        P(),
        P("ctx", "dp", "tensor"),
        P("ctx", "dp", "tensor", None),
        P("tensor", "ctx"),
    )
    return jax.shard_map(
        local, mesh=mesh, in_specs=placed, out_specs=P("tensor", "dp", "ctx"), check_vma=False
    )
```

profile of v0, /device:TPU:0, one launch (start us, length us, event | category | flops | bytes accessed | tf_op | source)
XLA Modules:
  0.0 379.5 jit_solution(5068524759064175050)
XLA Ops:
  6.5 0.9 reshape.249
  7.4 1.1 convert_reduce_fusion
  8.5 0.1 add.129
  8.6 0.1 fusion.63
  8.7 0.0 copy-start.2
  8.7 32.8 %gather_fusion.1 = s32[4096]{0:T(1024)S(1)} fusion(s32[16,1024]{1,0:T(8,128)S(1)} %reshape.249, s32[4096]{0:T(1024)S(1)} %bitcast.150), kind=kCustom, calls=%fused_computation.1 | custom fusion | bytes 65536 | tf_op jit(solution)/shard_map/jit(take_along_axis)/gather | solution.py:21
  41.5 0.1 select_subtract_fusion
  41.6 0.1 reduce_sum.68
  41.6 0.1 iota_compare_fusion.3
  41.7 0.1 compare_select_fusion.3
  41.8 3.7 fusion.20
  45.5 2.4 broadcast_in_dim.46
  47.9 5.0 %scatter_fusion = bf16[8,4,256,256]{3,2,1,0:T(8,128)(2,1)} fusion(bf16[8,4,256,256]{3,2,1,0:T(8,128)(2,1)} %broadcast_in_dim.46, s32[4]{0:T(128)S(1)} %compare_select_fusion.3, bf16[4,4,256,256]{3,2,1,0:T(8,128)(2,1)S(1)} %bitcast.153), kind=kCustom, calls=%fused_computation.2 | custom fusion | bytes 6291472 | tf_op jit(solution)/shard_map/scatter | solution.py:105
  52.9 7.3 %all-to-all-start = ((bf16[8,4,256,256]{3,2,1,0:T(8,128)(2,1)}), bf16[8,4,256,256]{3,2,1,0:T(8,128)(2,1)}, u32[]{:S(2)}, u32[]{:S(2)}) async-start(bf16[8,4,256,256]{3,2,1,0:T(8,128)(2,1)} %scatter_fusion), calls=%async_computation | async-start | bytes 8388608 | tf_op jit(solution)/shard_map/all_to_all | solution.py:113
  60.2 93.3 %all-to-all-done = bf16[8,4,256,256]{3,2,1,0:T(8,128)(2,1)} async-done(((bf16[8,4,256,256]{3,2,1,0:T(8,128)(2,1)}), bf16[8,4,256,256]{3,2,1,0:T(8,128)(2,1)}, u32[]{:S(2)}, u32[]{:S(2)}) %all-to-all-start) | async-done | bytes 4194336 | tf_op jit(solution)/shard_map/all_to_all | solution.py:113
  153.5 4.6 %copy.32 = bf16[8,4,256,256]{3,0,2,1:T(8,128)(2,1)S(1)} copy(bf16[8,4,256,256]{3,2,1,0:T(8,128)(2,1)} %all-to-all-done) | data formatting | bytes 8388608 | tf_op jit(solution)/shard_map/all_to_all | solution.py:113
  158.1 0.3 select_bitcast_fusion.1
  158.4 0.0 copy-start.1
  158.4 1.8 copy.34
  160.2 1.5 collective-permute-start
  161.8 1.2 scatter_custom_fusion.1
  162.9 3.6 all-to-all-start.1
  166.6 0.2 all-gather.2.cloned.1.call-start
  166.8 0.6 collective-permute-start.4
  167.4 0.6 compare_select_fusion.2
  170.6 0.5 copy.33
  171.1 37.1 %collective-permute-done = bf16[4,1024,256]{2,1,0:T(8,128)(2,1)} collective-permute-done((bf16[4,1024,256]{2,1,0:T(8,128)(2,1)}, bf16[4,1024,256]{2,1,0:T(8,128)(2,1)}, u32[]{:S(2)}, u32[]{:S(2)}) %collective-permute-start) | collective-permute-done | bytes 2097184 | tf_op jit(solution)/shard_map/ppermute | solution.py:10
  208.2 1.8 bitcast_select_fusion
  210.0 0.4 collective-permute-start.1
  210.4 0.1 iota_compare_fusion.2
  210.4 0.1 copy.37
  210.5 0.1 broadcast_bitcast_fusion
  210.6 1.8 collective-permute-start.2
  212.4 42.3 %collective-permute-done.2 = bf16[4,1024]{1,0:T(4,128)(2,1)S(1)} collective-permute-done((bf16[4,1024]{1,0:T(4,128)(2,1)S(1)}, bf16[4,1024]{1,0:T(4,128)(2,1)S(1)}, u32[]{:S(2)}, u32[]{:S(2)}) %collective-permute-start.2) | collective-permute-done | bytes 8224 | tf_op jit(solution)/shard_map/ppermute | solution.py:10
  254.7 1.5 collective-permute-start.3
  256.2 0.1 iota_compare_fusion.1
  256.4 2.0 collective-permute-done.3
  258.5 0.1 maximum_select_fusion
  258.6 0.4 fusion.81
  259.0 0.4 fusion.82
  259.4 2.8 bitcast_reduce_fusion.1
  262.2 0.3 fusion.52
  262.5 0.4 fusion.40
  262.9 4.8 %fusion.5 = (f32[32,4,8]{0,2,1:T(8,128)S(1)}, f32[32,4,8]{0,2,1:T(8,128)S(1)}, f32[4,2048,32,8]{1,2,3,0:T(8,128)S(1)}) fusion(f32[4,2048,32,8]{1,2,3,0:T(8,128)S(1)} %get-tuple-element.16, f32[32,4,8]{0,2,1:T(8,128)S(1)} %max.24, pred[4,2048]{1,0:T(4,128)(4,1)S(1)} %maximum_compare_fusion, bf16[32,4,8,128]{3,2,1,0:T(8,128)(2,1)S(1)} %bitcast.164, ...), kind=kOutput, calls=%fused_computation.15 | convolution fusion | flops 555743232 | bytes 21254144 | tf_op jit(solution)/shard_map/rkgd,knd->rkgn/dot_general | solution.py:42
  267.8 0.3 fusion.50
  268.1 0.4 fusion.42
  268.5 3.1 fusion.30
  271.6 0.3 copy.41
  271.9 0.3 copy.90
  272.3 2.1 fusion.7
  274.3 3.1 fusion.36
  277.5 0.3 copy.44
  277.8 0.3 copy.89
  278.1 0.1 pad_maximum_fusion.1
  278.2 0.1 copy.45
  278.3 0.3 div.22
  278.6 1.4 fusion.39
  280.1 0.0 all-gather.2.cloned.1.call-update
  280.1 0.3 reduce-scatter.2.cloned.1.call-start
  280.4 74.6 %all-gather.2.cloned.1.call-done = bf16[512,4096]{1,0:T(8,128)(2,1)} async-done(((bf16[64,4096]{1,0:T(8,128)(2,1)}), bf16[512,4096]{1,0:T(8,128)(2,1)}) %all-gather.2.cloned.1.call-update) | async-done | bytes 4194320 | tf_op jit(solution)/shard_map/all_gather | solution.py:150
  354.9 9.1 %fusion.83 = bf16[512,1024]{1,0:T(8,128)(2,1)S(1)} fusion(bf16[512,4096]{1,0:T(8,128)(2,1)} %all-gather.2.cloned.1.call-done, bf16[4096,1024]{1,0:T(8,128)(2,1)} %param.11), kind=kOutput, calls=%fused_computation.119 | convolution fusion | flops 4294967296 | bytes 13631488 | tf_op jit(solution)/shard_map/dot_general | solution.py:149
  364.1 1.6 gather_fusion
  365.7 0.0 reduce-scatter.2.cloned.1.call-update
  365.7 7.0 %reduce-scatter.2.cloned.1.call-done = bf16[4,64,1024]{2,1,0:T(8,128)(2,1)} async-done(((bf16[8,64,1024]{2,1,0:T(8,128)(2,1)}), bf16[4,64,1024]{2,1,0:T(8,128)(2,1)}) %reduce-scatter.2.cloned.1.call-update) | async-done | bytes 524304 | tf_op jit(solution)/shard_map/reduce_scatter | solution.py:155
  (27 shorter events, 0.3 us)
Async XLA Ops:
  8.7 33.1 %copy-start.2 = (s32[8]{0:T(128)S(1)}, s32[8]{0:T(128)}, u32[]{:S(2)}) copy-start(s32[8]{0:T(128)} %param.8) | copy-start | bytes 100
  52.9 100.5 %all-to-all-start = ((bf16[8,4,256,256]{3,2,1,0:T(8,128)(2,1)}), bf16[8,4,256,256]{3,2,1,0:T(8,128)(2,1)}, u32[]{:S(2)}, u32[]{:S(2)}) async-start(bf16[8,4,256,256]{3,2,1,0:T(8,128)(2,1)} %scatter_fusion), calls=%async_computation | async-start | bytes 8388608 | tf_op jit(solution)/shard_map/all_to_all | solution.py:113
  158.4 8.4 %copy-start.1 = (bf16[1,64,4,256]{3,2,1,0:T(4,128)(2,1)S(1)}, bf16[1,64,4,256]{3,2,1,0:T(4,128)(2,1)}, u32[]{:S(2)}) copy-start(bf16[1,64,4,256]{3,2,1,0:T(4,128)(2,1)} %param.10) | copy-start | bytes 393220
  158.4 12.2 %copy-start = (bf16[1,64,4096]{2,1,0:T(8,128)(2,1)S(1)}, bf16[1,64,4096]{2,1,0:T(8,128)(2,1)}, u32[]{:S(2)}) copy-start(bf16[1,64,4096]{2,1,0:T(8,128)(2,1)} %param.9) | copy-start | bytes 1572868
  160.2 47.9 %collective-permute-start = (bf16[4,1024,256]{2,1,0:T(8,128)(2,1)}, bf16[4,1024,256]{2,1,0:T(8,128)(2,1)}, u32[]{:S(2)}, u32[]{:S(2)}) collective-permute-start(bf16[4,1024,256]{2,1,0:T(8,128)(2,1)} %bitcast.8), channel_id=1, source_target_pairs={{0,1},{1,0},{2,3},{3,2},{4,5},{5,4},{6,7},{7,6},{8,9},{9,8},{10,11... | collective-permute-start | bytes 6291464 | tf_op jit(solution)/shard_map/ppermute | solution.py:10
  162.9 47.5 %all-to-all-start.1 = ((s32[8,1,4]{2,1,0:T(1,128)}), s32[8,1,4]{2,1,0:T(1,128)S(1)}, u32[]{:S(2)}, u32[]{:S(2)}) async-start(s32[8,1,4]{2,1,0:T(1,128)} %bitcast.36), calls=%async_computation.1 | async-start | bytes 8192 | tf_op jit(solution)/shard_map/all_to_all | solution.py:114
  166.6 188.4 %all-gather.2.cloned.1.call-start = ((), (), s32[]{:S(2)}) async-start(), calls=%async_computation.3 | async-start | bytes 4718592 | tf_op jit(solution)/shard_map/all_gather | solution.py:150
  166.8 91.6 %collective-permute-start.4 = (bf16[64,4,256]{2,0,1:T(8,128)(2,1)S(1)}, bf16[64,4,256]{2,0,1:T(8,128)(2,1)S(1)}, u32[]{:S(2)}, u32[]{:S(2)}) collective-permute-start(bf16[64,4,256]{2,0,1:T(8,128)(2,1)S(1)} %bitcast.161), channel_id=1, source_target_pairs={{0,1},{1,0},{2,3},{3,2},{4,5},{5,4},{6,7},{7,6},{8,9},{9,8},{10,11... | collective-permute-start | bytes 393224 | tf_op jit(solution)/shard_map/ppermute | solution.py:10
  210.0 49.4 %collective-permute-start.1 = (bf16[4,1024,256]{2,1,0:T(8,128)(2,1)S(1)}, bf16[4,1024,256]{2,1,0:T(8,128)(2,1)}, u32[]{:S(2)}, u32[]{:S(2)}) collective-permute-start(bf16[4,1024,256]{2,1,0:T(8,128)(2,1)S(1)} %bitcast_select_fusion), channel_id=1, source_target_pairs={{0,1},{1,0},{2,3},{3,2},{4,5},{5,4},{6,7},{7,6},{8,9},{9,8},{10,11... | collective-permute-start | bytes 6291464 | tf_op jit(solution)/shard_map/ppermute | solution.py:10
  210.6 44.1 %collective-permute-start.2 = (bf16[4,1024]{1,0:T(4,128)(2,1)S(1)}, bf16[4,1024]{1,0:T(4,128)(2,1)S(1)}, u32[]{:S(2)}, u32[]{:S(2)}) collective-permute-start(bf16[4,1024]{1,0:T(4,128)(2,1)S(1)} %broadcast_select_fusion), channel_id=1, source_target_pairs={{0,1},{1,0},{2,3},{3,2},{4,5},{5,4},{6,7},{7,6},{8,9},{9,8},{10,11... | collective-permute-start | bytes 24584 | tf_op jit(solution)/shard_map/ppermute | solution.py:10
  254.7 3.7 collective-permute-start.3
  280.1 92.6 %reduce-scatter.2.cloned.1.call-start = ((), (), s32[]{:S(2)}) async-start(), calls=%async_computation.4 | async-start | bytes 1572864 | tf_op jit(solution)/shard_map/reduce_scatter | solution.py:155
Sparse Core Ops, SparseCore 0:
  280.2 74.6 all-gather.1
  365.8 6.7 reduce-scatter.1
where the time goes:
time: 380 us; the launch traced here: 379 us
  waiting for transfers between devices  256 us (67%)
  local copies, waits for them, and re-layouts  51.8 us (14%)
  matrix products  28.1 us (7%)
  starting transfers between devices  17.1 us (5%)
  between operations  16.2 us (4%)
  other arithmetic  9.96 us (3%)
    all_to_all x1, waiting for transfers between devices, local(): lax.all_to_all(buffer, 'ctx', split_axis=0, concat_axis=0, tiled=True)  93.3 us
    ppermute x5, waiting for transfers between devices, swapped(): lax.ppermute(array, axis, [(i, i ^ 1 << distance) for i in range(lax.axis...  81.4 us
    all_gather x1, waiting for transfers between devices, local(): lax.all_gather(head_out, 'ctx', axis=0, tiled=True)  74.6 us
    gather x2, local copies, waits for them, and re-layouts, block_rows_of(): places = jnp.take_along_axis(kept_lists, rank_ids, axis=1) - block_start  32.8 us
    dot_general x1, matrix products, local(): jnp.dot(lax.all_gather(head_out, 'ctx', axis=0, tiled=True), out_weight,...  9.14 us
    dot_general x2, matrix products, attend_rows(): jnp.einsum('rkgd,knd->rkgn', query, kept_rows[:, :, :head_dim], preferred...  7.67 us
  transfers between devices with their start and end apart: 9, of which 6 were waited for; matrix products, arithmetic and copies ran while one was open for 1% of the time, Pallas kernels for 0%

commit v1 on v0

--- a/solution.py
+++ b/solution.py
@@ -1,6 +1,11 @@
+import functools
+import math
+
 import jax
 import jax.numpy as jnp
 from jax import lax
+from jax.experimental import pallas as pl
+from jax.experimental.pallas import tpu as pltpu
 from jax.sharding import PartitionSpec as P
 
 neg_large = -1e30
@@ -83,7 +88,7 @@
     return tuple((jnp.concatenate([first[index], second[index]], axis=0) for index in range(3)))
 
 
-def local(cache, kept, assign, queries, new_kv, out_weight):
+def local_by_rows(cache, kept, assign, queries, new_kv, out_weight):
     ctx_count = lax.axis_size("ctx")
     ctx_id = lax.axis_index("ctx")
     dp_id = lax.axis_index("dp")
@@ -157,6 +162,227 @@
     )
 
 
+def select_kernel(start_ref, kept_ref, cache_ref, out_ref):
+    start = start_ref[0]
+    kept = kept_ref[0]
+    total = kept.shape[1]
+    spots = cache_ref.shape[1]
+    capacity = out_ref.shape[1]
+    first = jnp.sum((kept < start).astype(jnp.int32))
+    wide = jnp.broadcast_to(kept, (8, total))
+    places = pltpu.roll(wide, lax.rem(total - first, total), 1)[:1, :capacity] - start
+    spot_ids = lax.broadcasted_iota(jnp.int32, (spots, capacity), 0)
+    chooser = (spot_ids == places).astype(jnp.float32).astype(jnp.bfloat16)
+    picked = lax.dot_general(
+        chooser, cache_ref[0], (((0,), (0,)), ((), ())), preferred_element_type=jnp.float32
+    )
+    out_ref[0] = picked.astype(out_ref.dtype)
+
+
+def select_rows(flat_cache, kept_lists, block_start, capacity):
+    lists, spots, width = flat_cache.shape
+    total = kept_lists.shape[1]
+    return pl.pallas_call(
+        select_kernel,
+        out_shape=jax.ShapeDtypeStruct((lists, capacity, width), flat_cache.dtype),
+        grid_spec=pltpu.PrefetchScalarGridSpec(
+            num_scalar_prefetch=1,
+            grid=(lists,),
+            in_specs=[
+                pl.BlockSpec((1, 1, total), lambda i, s: (i, 0, 0)),
+                pl.BlockSpec((1, spots, width), lambda i, s: (i, 0, 0)),
+            ],
+            out_specs=pl.BlockSpec((1, capacity, width), lambda i, s: (i, 0, 0)),
+        ),
+    )(block_start.reshape(1), kept_lists.reshape(lists, 1, total), flat_cache)
+
+
+def arrange_kernel(groups, order_ref, dp_ref, mine_ref, got_ref, out_ref):
+    from_mine = order_ref[pl.program_id(0)] // groups == dp_ref[0]
+
+    @pl.when(from_mine)
+    def _():
+        out_ref[...] = mine_ref[...]
+
+    @pl.when(jnp.logical_not(from_mine))
+    def _():
+        out_ref[...] = got_ref[...]
+
+
+def arrange(mine, got, order, dp_id):
+    groups, heads, capacity, width = mine.shape
+    block = (1, heads, capacity, width)
+
+    def source(i, order_ref, dp_ref):
+        return (order_ref[i] % groups, 0, 0, 0)
+
+    return pl.pallas_call(
+        functools.partial(arrange_kernel, groups),
+        out_shape=jax.ShapeDtypeStruct((order.shape[0], heads, capacity, width), mine.dtype),
+        grid_spec=pltpu.PrefetchScalarGridSpec(
+            num_scalar_prefetch=2,
+            grid=(order.shape[0],),
+            in_specs=[pl.BlockSpec(block, source), pl.BlockSpec(block, source)],
+            out_specs=pl.BlockSpec(block, lambda i, a, b: (i, 0, 0, 0)),
+        ),
+    )(order, dp_id.reshape(1), mine, got)
+
+
+def attend_kernel(q_ref, rows_ref, bias_ref, new_ref, out_ref):
+    blocks, _, capacity, width = rows_ref.shape
+    hd = width // 2
+    rows = q_ref.shape[0]
+    q = jnp.concatenate([q_ref[:, :hd], q_ref[:, hd:]], axis=0)
+    keys = rows_ref[:, 0, :, :hd].reshape(blocks * capacity, hd)
+    values = rows_ref[:, 0, :, hd:].reshape(blocks * capacity, hd)
+    new_keys = new_ref[0, :, :hd]
+    new_values = new_ref[0, :, hd:]
+    scale = hd**-0.5 * math.log2(math.e)
+    dims = (((1,), (1,)), ((), ()))
+    kept_scores = lax.dot_general(q, keys, dims, preferred_element_type=jnp.float32) * scale
+    kept_scores = kept_scores + bias_ref[0]
+    new_scores = lax.dot_general(q, new_keys, dims, preferred_element_type=jnp.float32) * scale
+    row_ids = lax.rem(lax.broadcasted_iota(jnp.int32, new_scores.shape, 0), rows)
+    key_ids = lax.broadcasted_iota(jnp.int32, new_scores.shape, 1)
+    new_scores = jnp.where(key_ids <= row_ids, new_scores, neg_large)
+    top = jnp.maximum(
+        jnp.max(kept_scores, axis=1, keepdims=True), jnp.max(new_scores, axis=1, keepdims=True)
+    )
+    kept_weights = jnp.exp2(kept_scores - top)
+    new_weights = jnp.exp2(new_scores - top)
+    total = jnp.sum(kept_weights, axis=1, keepdims=True) + jnp.sum(new_weights, axis=1, keepdims=True)
+    weighted = jnp.dot(
+        kept_weights.astype(jnp.bfloat16), values, preferred_element_type=jnp.float32
+    ) + jnp.dot(new_weights.astype(jnp.bfloat16), new_values, preferred_element_type=jnp.float32)
+    result = (weighted / total).astype(out_ref.dtype)
+    out_ref[:, :hd] = result[:rows]
+    out_ref[:, hd:] = result[rows:]
+
+
+def attend_heads(query, received, bias, new_rows, per_group):
+    rows, columns = query.shape
+    blocks, heads, capacity, width = received.shape
+    hd = width // 2
+    pairs = per_group // 2
+    return pl.pallas_call(
+        attend_kernel,
+        out_shape=jax.ShapeDtypeStruct(query.shape, query.dtype),
+        grid=(heads, pairs),
+        in_specs=[
+            pl.BlockSpec((rows, 2 * hd), lambda h, j: (0, h * pairs + j)),
+            pl.BlockSpec((blocks, 1, capacity, width), lambda h, j: (0, h, 0, 0)),
+            pl.BlockSpec((1, 1, blocks * capacity), lambda h, j: (h, 0, 0)),
+            pl.BlockSpec((1, rows, width), lambda h, j: (h, 0, 0)),
+        ],
+        out_specs=pl.BlockSpec((rows, 2 * hd), lambda h, j: (0, h * pairs + j)),
+        compiler_params=pltpu.CompilerParams(vmem_limit_bytes=48 * 1024 * 1024),
+    )(query, received, bias, new_rows)
+
+
+def project_kernel(assign_ref, heads_ref, weight_ref, out_ref, lhs):
+    prompts, rows, _ = heads_ref.shape
+
+    @pl.when(pl.program_id(0) == 0)
+    def _():
+        for p in range(prompts):
+            lhs[p * rows : (p + 1) * rows] = heads_ref[assign_ref[p]]
+
+    product = jnp.dot(lhs[...], weight_ref[...], preferred_element_type=jnp.float32)
+    out_ref[...] = product.astype(out_ref.dtype).reshape(out_ref.shape)
+
+
+def project(gathered, out_weight, assign):
+    prompts, rows, depth = gathered.shape
+    columns = out_weight.shape[1]
+    tile = min(256, columns)
+    return pl.pallas_call(
+        project_kernel,
+        out_shape=jax.ShapeDtypeStruct((prompts, rows, columns), gathered.dtype),
+        grid_spec=pltpu.PrefetchScalarGridSpec(
+            num_scalar_prefetch=1,
+            grid=(columns // tile,),
+            in_specs=[
+                pl.BlockSpec((prompts, rows, depth), lambda i, a: (0, 0, 0)),
+                pl.BlockSpec((depth, tile), lambda i, a: (0, i)),
+            ],
+            out_specs=pl.BlockSpec((prompts, rows, tile), lambda i, a: (0, 0, i)),
+            scratch_shapes=[pltpu.VMEM((prompts * rows, depth), gathered.dtype)],
+        ),
+        compiler_params=pltpu.CompilerParams(vmem_limit_bytes=48 * 1024 * 1024),
+    )(assign, gathered, out_weight)
+
+
+def in_dp_order(own, other, dp_id, axis):
+    return jnp.where(
+        dp_id == 0,
+        jnp.concatenate([own, other], axis=axis),
+        jnp.concatenate([other, own], axis=axis),
+    )
+
+
+def halves_of(array, dp_id, axis):
+    size = array.shape[axis] // 2
+    mine = lax.dynamic_slice_in_dim(array, dp_id * size, size, axis)
+    theirs = lax.dynamic_slice_in_dim(array, (1 - dp_id) * size, size, axis)
+    return mine, theirs
+
+
+def prepare(cache, kept, assign, queries, new_kv):
+    ctx_count = lax.axis_size("ctx")
+    ctx_id = lax.axis_index("ctx")
+    dp_id = lax.axis_index("dp")
+    groups, kv_here, ctx_dev, width = cache.shape
+    total = kept.shape[2]
+    prompts = assign.shape[0]
+    slots = jnp.arange(prompts, dtype=jnp.int32)
+    order = jnp.sum(jnp.where(assign[None, :] == slots[:, None], slots[None, :], 0), axis=1)
+    edges = ctx_dev * jnp.arange(ctx_count + 1, dtype=jnp.int32)
+    below = jnp.sum((kept[:, :, None, :] < edges[:, None]).astype(jnp.int32), axis=3)
+    counts = below[:, :, 1:] - below[:, :, :-1]
+    counts_mine, counts_theirs = halves_of(counts, dp_id, 1)
+    query_mine, query_theirs = halves_of(queries[0], dp_id, 1)
+    new_mine, new_theirs = halves_of(new_kv[0], dp_id, 1)
+    counts_got, query_got, new_got = swapped((counts_theirs, query_theirs, new_theirs), "dp", 0)
+    all_counts = in_dp_order(counts_mine, counts_got, dp_id, 0)
+    query = in_dp_order(query_mine, query_got, dp_id, 0)
+    new_rows = jnp.transpose(in_dp_order(new_mine, new_got, dp_id, 0), (1, 0, 2))
+    is_here = (assign == ctx_id).astype(jnp.int32)
+    slot_counts = jnp.sum(all_counts * is_here[:, None, None], axis=0)
+    capacity = ctx_dev // 2
+    offsets = jnp.arange(capacity, dtype=jnp.int32)
+    bias = jnp.where(offsets < slot_counts[:, :, None], 0.0, neg_large).astype(jnp.float32)
+    bias = bias.reshape(bias.shape[0], 1, ctx_count * capacity)
+    return order, query, new_rows, bias
+
+
+def local(cache, kept, assign, queries, new_kv, out_weight):
+    groups, kv_here, ctx_dev, width = cache.shape
+    if kv_here % 2:
+        return local_by_rows(cache, kept, assign, queries, new_kv, out_weight)
+    ctx_id = lax.axis_index("ctx")
+    dp_id = lax.axis_index("dp")
+    capacity = ctx_dev // 2
+    per_group = queries.shape[2] // (kv_here * (width // 2))
+    order, query, new_rows, bias = prepare(cache, kept, assign, queries, new_kv)
+    picked = select_rows(
+        cache.reshape(groups * kv_here, ctx_dev, width),
+        kept.reshape(groups * kv_here, kept.shape[2]),
+        ctx_id * ctx_dev,
+        capacity,
+    ).reshape(groups, kv_here, capacity, width)
+    picked_mine, picked_theirs = halves_of(picked, dp_id, 1)
+    picked_got = swapped(picked_theirs, "dp", 0)
+    buffer = arrange(picked_mine, picked_got, order, dp_id)
+    received = lax.all_to_all(buffer, "ctx", split_axis=0, concat_axis=0, tiled=True)
+    head_out = attend_heads(query, received, bias, new_rows, per_group)
+    out_mine, out_theirs = halves_of(head_out, dp_id, 0)
+    out_got = swapped(out_theirs, "dp", 0)
+    own_rows = in_dp_order(out_mine, out_got, dp_id, 1)
+    gathered = lax.all_gather(own_rows, "ctx", axis=0)
+    partials = project(gathered, out_weight, assign)
+    return lax.psum_scatter(partials, "tensor", scatter_dimension=0, tiled=True)
+
+
 def solution(mesh):
     placed = (
         P("dp", "tensor", "ctx", None),

time: 380 us -> 229 us (0.60)
  waiting for transfers between devices: 256 us -> 149 us
  local copies, waits for them, and re-layouts: 51.8 us -> 8.75 us
  Pallas kernels: 0 us -> 39.2 us
  matrix products: 28.1 us -> 0 us
  other arithmetic: 9.96 us -> 3.67 us
    all_to_all x1, waiting for transfers between devices: 93.3 us -> 34.6 us  [local(): lax.all_to_all(buffer, 'ctx', split_axis=0, concat_axis=0, tiled=True)]
    ppermute x5, waiting for transfers between devices: 81.4 us -> 32.9 us  [swapped(): lax.ppermute(array, axis, [(i, i ^ 1 << distance) for i in range(lax.axis...]
    pallas_call x0 -> x4, Pallas kernels: none -> 39.2 us  [the longest x1 13.5 us: select_rows(): pl.pallas_call(select_kernel, out_shape=jax.ShapeDtypeStruct((lists, capa...]
    gather x3 -> x0, local copies, waits for them, and re-layouts: 34.4 us -> none  [the longest x2 32.8 us: block_rows_of(): places = jnp.take_along_axis(kept_lists, rank_ids, axis=1) - block_start]
    dot_general x10 -> x0, matrix products: 28.1 us -> none  [the longest x1 9.14 us: local(): jnp.dot(lax.all_gather(head_out, 'ctx', axis=0, tiled=True), out_weight,...]
    scatter x1 -> x0, local copies, waits for them, and re-layouts: 5.03 us -> none  [local(): jnp.zeros((ctx_count, kv_here, capacity, row_width), cache.dtype)]
    all_to_all x2 -> x0, local copies, waits for them, and re-layouts: 4.67 us -> none  [the longest x1 4.59 us: local(): lax.all_to_all(buffer, 'ctx', split_axis=0, concat_axis=0, tiled=True)]
  transfers between devices with their start and end apart: 9 -> 8, of which waited for: 6 -> 7; matrix products, arithmetic and copies ran while one was open for 1% -> 1% of each run, Pallas kernels for 0% -> 0%
where the time goes in v1:
time: 229 us; the launch traced here: 228 us
  waiting for transfers between devices  149 us (65%)
  Pallas kernels  39.2 us (17%)
  starting transfers between devices  14.4 us (6%)
  between operations  13.5 us (6%)
  local copies, waits for them, and re-layouts  8.75 us (4%)
  other arithmetic  3.67 us (2%)
    all_gather x1, waiting for transfers between devices, local(): gathered = lax.all_gather(own_rows, 'ctx', axis=0)  74.4 us
    all_to_all x1, waiting for transfers between devices, local(): lax.all_to_all(buffer, 'ctx', split_axis=0, concat_axis=0, tiled=True)  34.6 us
    ppermute x5, waiting for transfers between devices, swapped(): lax.ppermute(array, axis, [(i, i ^ 1 << distance) for i in range(lax.axis...  32.9 us
    pallas_call x1, Pallas kernels, select_rows(): pl.pallas_call(select_kernel, out_shape=jax.ShapeDtypeStruct((lists, capa...  13.5 us
    pallas_call x1, Pallas kernels, attend_heads(): pl.pallas_call(attend_kernel, out_shape=jax.ShapeDtypeStruct(query.shape,...  10.2 us
    pallas_call x1, Pallas kernels, project(): pl.pallas_call(project_kernel, out_shape=jax.ShapeDtypeStruct((prompts, r...  8.71 us
    ppermute x5, starting transfers between devices, swapped(): lax.ppermute(array, axis, [(i, i ^ 1 << distance) for i in range(lax.axis...  8.19 us
    reduce_scatter x1, waiting for transfers between devices, local(): return lax.psum_scatter(partials, 'tensor', scatter_dimension=0, tiled=True)  6.95 us
  transfers between devices with their start and end apart: 8, of which 7 were waited for; matrix products, arithmetic and copies ran while one was open for 1% of the time, Pallas kernels for 0%

profile of v1, /device:TPU:0, one launch (start us, length us, event | category | flops | bytes accessed | tf_op | source)
XLA Modules:
  0.0 228.5 jit_solution(3070947216056808936)
XLA Ops:
  6.5 1.6 reshape_reshape.3.kept_ref
  8.1 13.5 %shard_map.64 = bf16[16,256,256]{2,1,0:T(8,128)(2,1)} custom-call(s32[1]{0:T(128)} %bitcast.3.start_ref, s32[16,1,1024]{2,1,0:T(1,128)} %reshape_reshape.3.kept_ref, bf16[16,512,256]{2,1,0:T(8,128)(2,1)} %bitcast.23), custom_call_target="tpu_custom_call" | custom-call | tf_op jit(solution)/shard_map/pallas_call | solution.py:185
  21.6 0.0 copy-start.1
  21.6 2.7 %constant_dynamic-slice_fusion.5 = (bf16[4,2,256,256]{3,2,1,0:T(8,128)(2,1)S(1)}, bf16[4,2,256,256]{3,2,1,0:T(8,128)(2,1)}) fusion(bf16[4,4,256,256]{3,2,1,0:T(8,128)(2,1)} %bitcast.22, s32[]{:T(128)S(6)} %select_n.83, s32[]{:T(128)S(6)} %select_n.82), kind=kLoop, calls=%fused_computation.23 | loop fusion | bytes 4194312 | tf_op jit(solution)/shard_map/dynamic_slice | solution.py:326
  24.3 3.0 %collective-permute-start.1 = (bf16[4,2,256,256]{3,2,1,0:T(8,128)(2,1)S(1)}, bf16[4,2,256,256]{3,2,1,0:T(8,128)(2,1)S(1)}, u32[]{:S(2)}, u32[]{:S(2)}) collective-permute-start(bf16[4,2,256,256]{3,2,1,0:T(8,128)(2,1)S(1)} %get-tuple-element.5), channel_id=1, source_target_pairs={{0,1},{1,0},{2,3},{3,2},{4,5},{5,4},{6,7},{7,6},{8,9},{9,8},{10,11... | collective-permute-start | bytes 3145736 | tf_op jit(solution)/shard_map/ppermute | solution.py:15
  27.2 0.0 copy-done.1
  27.2 0.6 select_reduce_fusion.order_ref
  27.9 22.5 %collective-permute-done.1.got_ref = bf16[4,2,256,256]{3,2,1,0:T(8,128)(2,1)S(1)} collective-permute-done((bf16[4,2,256,256]{3,2,1,0:T(8,128)(2,1)S(1)}, bf16[4,2,256,256]{3,2,1,0:T(8,128)(2,1)S(1)}, u32[]{:S(2)}, u32[]{:S(2)}) %collective-permute-start.1) | collective-permute-done | bytes 1048608 | tf_op jit(solution)/shard_map/ppermute | solution.py:15
  50.4 0.0 copy-start.2
  50.4 1.0 copy-done.2
  51.4 6.7 %shard_map.65 = bf16[8,2,256,256]{3,2,1,0:T(8,128)(2,1)} custom-call(s32[8]{0:T(128)} %select_reduce_fusion.order_ref, s32[1]{0:T(128)} %bitcast.2.dp_ref, bf16[4,2,256,256]{3,2,1,0:T(8,128)(2,1)} %get-tuple-element.6.mine_ref, bf16[4,2,256,256]{3,2,1,0:T(8,128)(2,1)} %copy-done.2), custom_call_target="tpu_custom_call" | custom-call | tf_op jit(solution)/shard_map/pallas_call | solution.py:219
  58.1 0.0 copy-start.4
  58.1 0.0 copy-start.6
  58.1 0.0 copy-start.3
  58.1 6.2 %all-to-all-start = ((bf16[8,2,256,256]{3,2,1,0:T(8,128)(2,1)}), bf16[8,2,256,256]{3,2,1,0:T(8,128)(2,1)S(1)}, u32[]{:S(2)}, u32[]{:S(2)}) async-start(bf16[8,2,256,256]{3,2,1,0:T(8,128)(2,1)} %shard_map.65), calls=%async_computation | async-start | bytes 4194304 | tf_op jit(solution)/shard_map/all_to_all | solution.py:376
  64.3 0.0 all-gather.2.cloned.1.call-start
  64.4 0.0 copy-done.4
  64.4 0.8 convert_reduce_fusion
  65.2 0.1 constant_dynamic-slice_fusion.4
  65.2 1.5 collective-permute-start.2
  66.7 0.0 copy-done.6
  66.8 0.1 constant_dynamic-slice_fusion.2
  66.9 0.6 collective-permute-start.3
  67.5 0.0 copy-done.3
  67.6 1.6 collective-permute-start
  69.1 0.1 copy.14
  69.3 0.0 collective-permute-done.2
  69.3 0.1 copy.15
  69.4 0.1 fusion.2
  69.5 0.1 lt.71
  69.6 2.4 %collective-permute-done.3 = bf16[64,2,256]{2,0,1:T(8,128)(2,1)S(1)} collective-permute-done((bf16[64,2,256]{2,0,1:T(8,128)(2,1)S(1)}, bf16[64,2,256]{2,0,1:T(8,128)(2,1)S(1)}, u32[]{:S(2)}, u32[]{:S(2)}) %collective-permute-start.3) | collective-permute-done | bytes 65568 | tf_op jit(solution)/shard_map/ppermute | solution.py:15
  72.0 3.1 %collective-permute-done = bf16[64,2048]{1,0:T(8,128)(2,1)S(1)} collective-permute-done((bf16[64,2048]{1,0:T(8,128)(2,1)S(1)}, bf16[64,2048]{1,0:T(8,128)(2,1)S(1)}, u32[]{:S(2)}, u32[]{:S(2)}) %collective-permute-start) | collective-permute-done | bytes 262176 | tf_op jit(solution)/shard_map/ppermute | solution.py:15
  75.1 0.0 copy-start.5
  75.1 0.7 copy-done.5
  75.9 1.2 maximum_select_fusion.q_ref
  77.1 34.6 %all-to-all-done.rows_ref = bf16[8,2,256,256]{3,2,1,0:T(8,128)(2,1)S(1)} async-done(((bf16[8,2,256,256]{3,2,1,0:T(8,128)(2,1)}), bf16[8,2,256,256]{3,2,1,0:T(8,128)(2,1)S(1)}, u32[]{:S(2)}, u32[]{:S(2)}) %all-to-all-start) | async-done | bytes 2097184 | tf_op jit(solution)/shard_map/all_to_all | solution.py:376
  111.7 10.2 %shard_map.66 = bf16[128,2048]{1,0:T(8,128)(2,1)S(1)} custom-call(bf16[128,2048]{1,0:T(8,128)(2,1)S(1)} %maximum_select_fusion.q_ref, bf16[8,2,256,256]{3,2,1,0:T(8,128)(2,1)S(1)} %all-to-all-done.rows_ref, f32[2,1,2048]{2,1,0:T(1,128)S(1)} %compare_select_fusion.bias_ref, bf16[2,128,256]{2,1,0:T(8,128)(2,1)S(1)} %fusion.new_ref), custom_call_target="tpu_custom_call" | custom-call | tf_op jit(solution)/shard_map/pallas_call | solution.py:267
  121.9 0.1 dynamic-slice_bitcast_fusion
  121.9 1.6 collective-permute-start.4
  123.5 4.9 %collective-permute-done.4 = bf16[64,2048]{1,0:T(8,128)(2,1)S(1)} collective-permute-done((bf16[64,2048]{1,0:T(8,128)(2,1)S(1)}, bf16[64,2048]{1,0:T(8,128)(2,1)S(1)}, u32[]{:S(2)}, u32[]{:S(2)}) %collective-permute-start.4) | collective-permute-done | bytes 262176 | tf_op jit(solution)/shard_map/ppermute | solution.py:15
  128.4 0.9 maximum_select_fusion.1
  129.3 0.0 all-gather.2.cloned.1.call-update
  129.3 0.0 reduce-scatter.2.cloned.1.call-start
  129.4 74.4 %all-gather.2.cloned.1.call-done.heads_ref = bf16[8,64,4096]{2,1,0:T(8,128)(2,1)} async-done(((bf16[1,64,4096]{2,1,0:T(8,128)(2,1)}), bf16[8,64,4096]{2,1,0:T(8,128)(2,1)}) %all-gather.2.cloned.1.call-update) | async-done | bytes 4194320 | tf_op jit(solution)/shard_map/all_gather | solution.py:381
  203.8 0.0 copy-start
  203.8 2.2 copy-done
  206.0 8.7 %shard_map.67 = bf16[8,64,1024]{2,1,0:T(8,128)(2,1)} custom-call(s32[8]{0:T(128)S(1)} %copy-done.1, bf16[8,64,4096]{2,1,0:T(8,128)(2,1)S(1)} %copy-done, bf16[4096,1024]{1,0:T(8,128)(2,1)} %weight_ref.1), custom_call_target="tpu_custom_call" | custom-call | tf_op jit(solution)/shard_map/pallas_call | solution.py:298
  214.7 0.0 reduce-scatter.2.cloned.1.call-update
  214.7 7.0 %reduce-scatter.2.cloned.1.call-done = bf16[4,64,1024]{2,1,0:T(8,128)(2,1)} async-done(((bf16[8,64,1024]{2,1,0:T(8,128)(2,1)}), bf16[4,64,1024]{2,1,0:T(8,128)(2,1)}) %reduce-scatter.2.cloned.1.call-update) | async-done | bytes 524304 | tf_op jit(solution)/shard_map/reduce_scatter | solution.py:383
  (11 shorter events, 0.2 us)
Async XLA Ops:
  21.6 5.6 %copy-start.1 = (s32[8]{0:T(128)S(1)}, s32[8]{0:T(128)}, u32[]{:S(2)}) copy-start(s32[8]{0:T(128)} %assign_ref.1) | copy-start | bytes 100
  24.3 26.1 %collective-permute-start.1 = (bf16[4,2,256,256]{3,2,1,0:T(8,128)(2,1)S(1)}, bf16[4,2,256,256]{3,2,1,0:T(8,128)(2,1)S(1)}, u32[]{:S(2)}, u32[]{:S(2)}) collective-permute-start(bf16[4,2,256,256]{3,2,1,0:T(8,128)(2,1)S(1)} %get-tuple-element.5), channel_id=1, source_target_pairs={{0,1},{1,0},{2,3},{3,2},{4,5},{5,4},{6,7},{7,6},{8,9},{9,8},{10,11... | collective-permute-start | bytes 3145736 | tf_op jit(solution)/shard_map/ppermute | solution.py:15
  50.4 1.0 copy-start.2
  58.1 6.2 %copy-start.4 = (s32[4,4,1024]{2,1,0:T(4,128)S(1)}, s32[4,4,1024]{2,1,0:T(4,128)}, u32[]{:S(2)}) copy-start(s32[4,4,1024]{2,1,0:T(4,128)} %param.7) | copy-start | bytes 196612
  58.1 8.6 %copy-start.6 = (bf16[1,64,4,256]{3,2,1,0:T(4,128)(2,1)S(1)}, bf16[1,64,4,256]{3,2,1,0:T(4,128)(2,1)}, u32[]{:S(2)}) copy-start(bf16[1,64,4,256]{3,2,1,0:T(4,128)(2,1)} %param.10) | copy-start | bytes 393220
  58.1 9.4 %copy-start.3 = (bf16[1,64,4096]{2,1,0:T(8,128)(2,1)S(1)}, bf16[1,64,4096]{2,1,0:T(8,128)(2,1)}, u32[]{:S(2)}) copy-start(bf16[1,64,4096]{2,1,0:T(8,128)(2,1)} %param.9) | copy-start | bytes 1572868
  58.1 53.5 %all-to-all-start = ((bf16[8,2,256,256]{3,2,1,0:T(8,128)(2,1)}), bf16[8,2,256,256]{3,2,1,0:T(8,128)(2,1)S(1)}, u32[]{:S(2)}, u32[]{:S(2)}) async-start(bf16[8,2,256,256]{3,2,1,0:T(8,128)(2,1)} %shard_map.65), calls=%async_computation | async-start | bytes 4194304 | tf_op jit(solution)/shard_map/all_to_all | solution.py:376
  64.3 139.5 %all-gather.2.cloned.1.call-start = ((), (), s32[]{:S(2)}) async-start(), calls=%async_computation.2 | async-start | bytes 4718592 | tf_op jit(solution)/shard_map/all_gather | solution.py:381
  65.2 4.0 %collective-permute-start.2 = (s32[4,2,8]{1,2,0:T(8,128)S(1)}, s32[4,2,8]{1,2,0:T(8,128)S(1)}, u32[]{:S(2)}, u32[]{:S(2)}) collective-permute-start(s32[4,2,8]{1,2,0:T(8,128)S(1)} %get-tuple-element.14), channel_id=1, source_target_pairs={{0,1},{1,0},{2,3},{3,2},{4,5},{5,4},{6,7},{7,6},{8,9},{9,8},{10,11... | collective-permute-start | bytes 776 | tf_op jit(solution)/shard_map/ppermute | solution.py:15
  66.9 5.1 %collective-permute-start.3 = (bf16[64,2,256]{2,0,1:T(8,128)(2,1)S(1)}, bf16[64,2,256]{2,0,1:T(8,128)(2,1)S(1)}, u32[]{:S(2)}, u32[]{:S(2)}) collective-permute-start(bf16[64,2,256]{2,0,1:T(8,128)(2,1)S(1)} %bitcast.26), channel_id=1, source_target_pairs={{0,1},{1,0},{2,3},{3,2},{4,5},{5,4},{6,7},{7,6},{8,9},{9,8},{10,11... | collective-permute-start | bytes 196616 | tf_op jit(solution)/shard_map/ppermute | solution.py:15
  67.6 7.6 %collective-permute-start = (bf16[64,2048]{1,0:T(8,128)(2,1)S(1)}, bf16[64,2048]{1,0:T(8,128)(2,1)S(1)}, u32[]{:S(2)}, u32[]{:S(2)}) collective-permute-start(bf16[64,2048]{1,0:T(8,128)(2,1)S(1)} %get-tuple-element.10), channel_id=1, source_target_pairs={{0,1},{1,0},{2,3},{3,2},{4,5},{5,4},{6,7},{7,6},{8,9},{9,8},{10,11... | collective-permute-start | bytes 786440 | tf_op jit(solution)/shard_map/ppermute | solution.py:15
  75.1 0.7 copy-start.5
  121.9 6.4 %collective-permute-start.4 = (bf16[64,2048]{1,0:T(8,128)(2,1)S(1)}, bf16[64,2048]{1,0:T(8,128)(2,1)S(1)}, u32[]{:S(2)}, u32[]{:S(2)}) collective-permute-start(bf16[64,2048]{1,0:T(8,128)(2,1)S(1)} %get-tuple-element.8), channel_id=1, source_target_pairs={{0,1},{1,0},{2,3},{3,2},{4,5},{5,4},{6,7},{7,6},{8,9},{9,8},{10,11... | collective-permute-start | bytes 786440 | tf_op jit(solution)/shard_map/ppermute | solution.py:15
  129.3 92.3 %reduce-scatter.2.cloned.1.call-start = ((), (), s32[]{:S(2)}) async-start(), calls=%async_computation.3 | async-start | bytes 1572864 | tf_op jit(solution)/shard_map/reduce_scatter | solution.py:383
  203.8 2.2 copy-start
Sparse Core Ops, SparseCore 0:
  129.4 74.2 all-gather.1
  214.8 6.7 reduce-scatter.1

commit v2 on v1

--- a/solution.py
+++ b/solution.py
@@ -9,6 +9,7 @@
 from jax.sharding import PartitionSpec as P
 
 neg_large = -1e30
+MESH = pl.DeviceIdType.MESH
 
 
 def swapped(array, axis, distance):
@@ -279,37 +280,209 @@
     )(query, received, bias, new_rows)
 
 
-def project_kernel(assign_ref, heads_ref, weight_ref, out_ref, lhs):
-    prompts, rows, _ = heads_ref.shape
-
-    @pl.when(pl.program_id(0) == 0)
+def gather_project_kernel(
+    assign_ref, heads_ref, weight_hbm, out_ref,
+    gat, weight, part, send_buf, recv_buf,
+    send, recv, y_send, core_send, core_recv, weight_sem,
+):
+    c = lax.axis_index("ctx")
+    t = lax.axis_index("tensor")
+    d = lax.axis_index("dp")
+    z, x = c // 2, c % 2
+    zs = gat.shape[1] // 2
+    rows = gat.shape[2]
+    tile = part.shape[3]
+    partner_x = z * 2 + 1 - x
+    kept = out_ref.shape[0]
+
+    load_weight = pltpu.make_async_copy(weight_hbm, weight, weight_sem)
+    load_weight.start()
+    barrier = pltpu.get_barrier_semaphore()
+    for target in ({"ctx": partner_x}, {"dp": 1 - d}, {"tensor": 1 - t}):
+        pl.semaphore_signal(barrier, inc=1, device_id=target, device_id_type=MESH)
+
+    @pl.when(z > 0)
     def _():
-        for p in range(prompts):
-            lhs[p * rows : (p + 1) * rows] = heads_ref[assign_ref[p]]
-
-    product = jnp.dot(lhs[...], weight_ref[...], preferred_element_type=jnp.float32)
-    out_ref[...] = product.astype(out_ref.dtype).reshape(out_ref.shape)
-
-
-def project(gathered, out_weight, assign):
-    prompts, rows, depth = gathered.shape
-    columns = out_weight.shape[1]
-    tile = min(256, columns)
+        pl.semaphore_signal(barrier, inc=1, device_id={"ctx": c - 2}, device_id_type=MESH)
+
+    @pl.when(z < zs - 1)
+    def _():
+        pl.semaphore_signal(barrier, inc=1, device_id={"ctx": c + 2}, device_id_type=MESH)
+
+    pl.semaphore_wait(barrier, 3 + (z > 0).astype(jnp.int32) + (z < zs - 1).astype(jnp.int32))
+
+    cols = (d, 1 - d)
+
+    def copy(piece, slot, channel):
+        ref = gat.at[cols[piece], slot]
+        target = (c + 2, c - 2, partner_x)[channel]
+        return pltpu.make_async_remote_copy(
+            src_ref=ref, dst_ref=ref, send_sem=send.at[piece, slot, channel],
+            recv_sem=recv.at[piece, slot], device_id={"ctx": target}, device_id_type=MESH,
+        )
+
+    def up(piece, slot):
+        @pl.when(z < zs - 1)
+        def _():
+            copy(piece, slot, 0).start()
+
+    def down(piece, slot):
+        @pl.when(z > 0)
+        def _():
+            copy(piece, slot, 1).start()
+
+    def arrived(piece, slot):
+        copy(piece, slot, 2).wait_recv()
+
+    y_copy = pltpu.make_async_remote_copy(
+        src_ref=heads_ref.at[pl.ds((1 - d) * rows, rows)], dst_ref=gat.at[d, c],
+        send_sem=y_send, recv_sem=recv.at[1, c], device_id={"dp": 1 - d}, device_id_type=MESH,
+    )
+    y_copy.start()
+    gat[d, c] = heads_ref[pl.ds(pl.multiple_of(d * rows, rows), rows)]
+    up(0, c)
+    down(0, c)
+    copy(0, c, 2).start()
+    arrived(1, c)
+    copy(1, c, 2).start()
+    up(1, c)
+    down(1, c)
+    arrived(1, partner_x)
+    up(1, partner_x)
+    down(1, partner_x)
+    for k in range(1, zs):
+        @pl.when(z >= k)
+        def _():
+            arrived(0, c - 2 * k)
+            up(0, c - 2 * k)
+            copy(0, c - 2 * k, 2).start()
+
+        @pl.when(z + k < zs)
+        def _():
+            arrived(0, c + 2 * k)
+            down(0, c + 2 * k)
+            copy(0, c + 2 * k, 2).start()
+
+        for base in (c, partner_x):
+            @pl.when(z >= k)
+            def _():
+                arrived(1, base - 2 * k)
+                up(1, base - 2 * k)
+
+            @pl.when(z + k < zs)
+            def _():
+                arrived(1, base + 2 * k)
+                down(1, base + 2 * k)
+
+    for zo in range(zs):
+        arrived(0, zo * 2 + 1 - x)
+    load_weight.wait()
+
+    slots = gat.shape[1]
+    depth = gat.shape[3]
+    tiles = part.shape[0]
+
+    def exchange(n):
+        return pltpu.make_async_remote_copy(
+            src_ref=send_buf.at[n], dst_ref=recv_buf.at[n], send_sem=core_send.at[n],
+            recv_sem=core_recv.at[n], device_id={"tensor": 1 - t}, device_id_type=MESH,
+        )
+
+    def tile_step(n, carry):
+        span = pl.ds(pl.multiple_of(n * tile, tile), tile)
+        product = jnp.dot(
+            gat[0].reshape(slots * rows, depth), weight[:depth, span], preferred_element_type=jnp.float32
+        ) + jnp.dot(
+            gat[1].reshape(slots * rows, depth), weight[depth:, span], preferred_element_type=jnp.float32
+        )
+        part[n] = product.reshape(slots, rows, tile)
+        for j in range(kept):
+            send_buf[n, j] = part[n, assign_ref[(1 - t) * kept + j]].astype(send_buf.dtype)
+        exchange(n).start()
+        return carry
+
+    lax.fori_loop(0, tiles, tile_step, 0)
+    for n in range(tiles):
+        exchange(n).wait_recv()
+        for j in range(kept):
+            total = part[n, assign_ref[t * kept + j]] + recv_buf[n, j].astype(jnp.float32)
+            out_ref[j, :, n * tile : (n + 1) * tile] = total.astype(out_ref.dtype)
+
+    y_copy.wait_send()
+    for n in range(tiles):
+        exchange(n).wait_send()
+    copy(0, c, 2).wait_send()
+    copy(1, c, 2).wait_send()
+
+    @pl.when(z < zs - 1)
+    def _():
+        copy(0, c, 0).wait_send()
+        copy(1, c, 0).wait_send()
+        copy(1, partner_x, 0).wait_send()
+
+    @pl.when(z > 0)
+    def _():
+        copy(0, c, 1).wait_send()
+        copy(1, c, 1).wait_send()
+        copy(1, partner_x, 1).wait_send()
+
+    for k in range(1, zs):
+        @pl.when(z >= k)
+        def _():
+            copy(0, c - 2 * k, 2).wait_send()
+
+            @pl.when(z < zs - 1)
+            def _():
+                copy(0, c - 2 * k, 0).wait_send()
+                copy(1, c - 2 * k, 0).wait_send()
+                copy(1, partner_x - 2 * k, 0).wait_send()
+
+        @pl.when(z + k < zs)
+        def _():
+            copy(0, c + 2 * k, 2).wait_send()
+
+            @pl.when(z > 0)
+            def _():
+                copy(0, c + 2 * k, 1).wait_send()
+                copy(1, c + 2 * k, 1).wait_send()
+                copy(1, partner_x + 2 * k, 1).wait_send()
+
+
+def gather_project(head_out, out_weight, assign):
+    slots = assign.shape[0]
+    rows, half_depth = head_out.shape[0] // 2, head_out.shape[1]
+    depth, columns = out_weight.shape
+    kept = slots // 2
+    tile = 256
+    tiles = columns // tile
+    kind = head_out.dtype
+    dma = pltpu.SemaphoreType.DMA
     return pl.pallas_call(
-        project_kernel,
-        out_shape=jax.ShapeDtypeStruct((prompts, rows, columns), gathered.dtype),
-        grid_spec=pltpu.PrefetchScalarGridSpec(
-            num_scalar_prefetch=1,
-            grid=(columns // tile,),
-            in_specs=[
-                pl.BlockSpec((prompts, rows, depth), lambda i, a: (0, 0, 0)),
-                pl.BlockSpec((depth, tile), lambda i, a: (0, i)),
-            ],
-            out_specs=pl.BlockSpec((prompts, rows, tile), lambda i, a: (0, 0, i)),
-            scratch_shapes=[pltpu.VMEM((prompts * rows, depth), gathered.dtype)],
+        gather_project_kernel,
+        out_shape=jax.ShapeDtypeStruct((kept, rows, columns), kind),
+        in_specs=[
+            pl.BlockSpec(memory_space=pltpu.SMEM),
+            pl.BlockSpec(memory_space=pltpu.VMEM),
+            pl.BlockSpec(memory_space=pl.ANY),
+        ],
+        out_specs=pl.BlockSpec(memory_space=pltpu.VMEM),
+        scratch_shapes=[
+            pltpu.VMEM((2, slots, rows, half_depth), kind),
+            pltpu.VMEM((depth, columns), kind),
+            pltpu.VMEM((tiles, slots, rows, tile), jnp.float32),
+            pltpu.VMEM((tiles, kept, rows, tile), kind),
+            pltpu.VMEM((tiles, kept, rows, tile), kind),
+            dma((2, slots, 3)),
+            dma((2, slots)),
+            dma,
+            dma((tiles,)),
+            dma((tiles,)),
+            dma,
+        ],
+        compiler_params=pltpu.CompilerParams(
+            collective_id=1, has_side_effects=True, vmem_limit_bytes=48 * 1024 * 1024
         ),
-        compiler_params=pltpu.CompilerParams(vmem_limit_bytes=48 * 1024 * 1024),
-    )(assign, gathered, out_weight)
+    )(assign, head_out, out_weight)
 
 
 def in_dp_order(own, other, dp_id, axis):
@@ -357,7 +530,7 @@
 
 def local(cache, kept, assign, queries, new_kv, out_weight):
     groups, kv_here, ctx_dev, width = cache.shape
-    if kv_here % 2:
+    if kv_here % 2 or lax.axis_size("ctx") != 8 or lax.axis_size("tensor") != 2:
         return local_by_rows(cache, kept, assign, queries, new_kv, out_weight)
     ctx_id = lax.axis_index("ctx")
     dp_id = lax.axis_index("dp")
@@ -375,12 +548,7 @@
     buffer = arrange(picked_mine, picked_got, order, dp_id)
     received = lax.all_to_all(buffer, "ctx", split_axis=0, concat_axis=0, tiled=True)
     head_out = attend_heads(query, received, bias, new_rows, per_group)
-    out_mine, out_theirs = halves_of(head_out, dp_id, 0)
-    out_got = swapped(out_theirs, "dp", 0)
-    own_rows = in_dp_order(out_mine, out_got, dp_id, 1)
-    gathered = lax.all_gather(own_rows, "ctx", axis=0)
-    partials = project(gathered, out_weight, assign)
-    return lax.psum_scatter(partials, "tensor", scatter_dimension=0, tiled=True)
+    return gather_project(head_out, out_weight, assign)
 
 
 def solution(mesh):

time: 229 us -> 177 us (0.77)
  waiting for transfers between devices: 149 us -> 62.7 us
  Pallas kernels: 39.2 us -> 90.4 us
  between operations: 13.5 us -> 0.13 us
    all_gather x1 -> x0, waiting for transfers between devices: 74.4 us -> none  [local(): gathered = lax.all_gather(own_rows, 'ctx', axis=0)]
    pallas_call x1, Pallas kernels: 8.71 us -> 59.9 us  [gather_project(): pl.pallas_call(gather_project_kernel, out_shape=jax.ShapeDtypeStruct((kep...]
    reduce_scatter x1 -> x0, waiting for transfers between devices: 6.95 us -> none  [local(): return lax.psum_scatter(partials, 'tensor', scatter_dimension=0, tiled=True)]
    ppermute x5 -> x4, waiting for transfers between devices: 32.9 us -> 26.4 us  [swapped(): lax.ppermute(array, axis, [(i, i ^ 1 << distance) for i in range(lax.axis...]
    ppermute x5 -> x4, starting transfers between devices: 8.19 us -> 6.65 us  [swapped(): lax.ppermute(array, axis, [(i, i ^ 1 << distance) for i in range(lax.axis...]
  transfers between devices with their start and end apart: 8 -> 5, of which waited for: 7 -> 3; matrix products, arithmetic and copies ran while one was open for 1% -> 2% of each run, Pallas kernels for 0% -> 0%
where the time goes in v2:
time: 177 us; the launch traced here: 176 us
  Pallas kernels  90.4 us (51%)
  waiting for transfers between devices  62.7 us (35%)
  starting transfers between devices  12.8 us (7%)
  local copies, waits for them, and re-layouts  7.32 us (4%)
  other arithmetic  2.75 us (2%)
    pallas_call x1, Pallas kernels, gather_project(): pl.pallas_call(gather_project_kernel, out_shape=jax.ShapeDtypeStruct((kep...  59.9 us
    all_to_all x1, waiting for transfers between devices, local(): lax.all_to_all(buffer, 'ctx', split_axis=0, concat_axis=0, tiled=True)  36.3 us
    ppermute x4, waiting for transfers between devices, swapped(): lax.ppermute(array, axis, [(i, i ^ 1 << distance) for i in range(lax.axis...  26.4 us
    pallas_call x1, Pallas kernels, select_rows(): pl.pallas_call(select_kernel, out_shape=jax.ShapeDtypeStruct((lists, capa...  13.5 us
    pallas_call x1, Pallas kernels, attend_heads(): pl.pallas_call(attend_kernel, out_shape=jax.ShapeDtypeStruct(query.shape,...  10.2 us
    pallas_call x1, Pallas kernels, arrange(): pl.pallas_call(functools.partial(arrange_kernel, groups), out_shape=jax.S...  6.71 us
    ppermute x4, starting transfers between devices, swapped(): lax.ppermute(array, axis, [(i, i ^ 1 << distance) for i in range(lax.axis...  6.65 us
    all_to_all x1, starting transfers between devices, local(): lax.all_to_all(buffer, 'ctx', split_axis=0, concat_axis=0, tiled=True)  6.17 us
  transfers between devices with their start and end apart: 5, of which 3 were waited for; matrix products, arithmetic and copies ran while one was open for 2% of the time, Pallas kernels for 0%

profile of v2, /device:TPU:0, one launch (start us, length us, event | category | flops | bytes accessed | tf_op | source)
XLA Modules:
  0.0 176.1 jit_solution(13029231238583962521)
XLA Ops:
  0.0 1.6 reshape_reshape.3.kept_ref
  1.6 13.5 %shard_map.64 = bf16[16,256,256]{2,1,0:T(8,128)(2,1)} custom-call(s32[1]{0:T(128)} %bitcast.3.start_ref, s32[16,1,1024]{2,1,0:T(1,128)} %reshape_reshape.3.kept_ref, bf16[16,512,256]{2,1,0:T(8,128)(2,1)} %bitcast.20), custom_call_target="tpu_custom_call" | custom-call | tf_op jit(solution)/shard_map/pallas_call | solution.py:186
  15.1 0.0 copy-start
  15.1 2.7 %constant_dynamic-slice_fusion.3 = (bf16[4,2,256,256]{3,2,1,0:T(8,128)(2,1)S(1)}, bf16[4,2,256,256]{3,2,1,0:T(8,128)(2,1)}) fusion(bf16[4,4,256,256]{3,2,1,0:T(8,128)(2,1)} %bitcast.19, s32[]{:T(128)S(6)} %select_n.61, s32[]{:T(128)S(6)} %select_n.60), kind=kLoop, calls=%fused_computation.19 | loop fusion | bytes 4194312 | tf_op jit(solution)/shard_map/dynamic_slice | solution.py:499
  17.8 3.0 %collective-permute-start.1 = (bf16[4,2,256,256]{3,2,1,0:T(8,128)(2,1)S(1)}, bf16[4,2,256,256]{3,2,1,0:T(8,128)(2,1)S(1)}, u32[]{:S(2)}, u32[]{:S(2)}) collective-permute-start(bf16[4,2,256,256]{3,2,1,0:T(8,128)(2,1)S(1)} %get-tuple-element.5), channel_id=1, source_target_pairs={{0,1},{1,0},{2,3},{3,2},{4,5},{5,4},{6,7},{7,6},{8,9},{9,8},{10,11... | collective-permute-start | bytes 3145736 | tf_op jit(solution)/shard_map/ppermute | solution.py:16
  20.7 0.0 copy-done
  20.7 0.6 select_reduce_fusion.order_ref
  21.4 22.5 %collective-permute-done.1.got_ref = bf16[4,2,256,256]{3,2,1,0:T(8,128)(2,1)S(1)} collective-permute-done((bf16[4,2,256,256]{3,2,1,0:T(8,128)(2,1)S(1)}, bf16[4,2,256,256]{3,2,1,0:T(8,128)(2,1)S(1)}, u32[]{:S(2)}, u32[]{:S(2)}) %collective-permute-start.1) | collective-permute-done | bytes 1048608 | tf_op jit(solution)/shard_map/ppermute | solution.py:16
  43.9 0.0 copy-start.1
  43.9 1.0 copy-done.1
  44.9 6.7 %shard_map.65 = bf16[8,2,256,256]{3,2,1,0:T(8,128)(2,1)} custom-call(s32[8]{0:T(128)} %select_reduce_fusion.order_ref, s32[1]{0:T(128)} %bitcast.2.dp_ref, bf16[4,2,256,256]{3,2,1,0:T(8,128)(2,1)} %get-tuple-element.6.mine_ref, bf16[4,2,256,256]{3,2,1,0:T(8,128)(2,1)} %copy-done.1), custom_call_target="tpu_custom_call" | custom-call | tf_op jit(solution)/shard_map/pallas_call | solution.py:220
  51.6 0.0 copy-start.2
  51.6 0.0 copy-start.5
  51.6 0.0 copy-start.3
  51.6 6.2 %all-to-all-start = ((bf16[8,2,256,256]{3,2,1,0:T(8,128)(2,1)}), bf16[8,2,256,256]{3,2,1,0:T(8,128)(2,1)S(1)}, u32[]{:S(2)}, u32[]{:S(2)}) async-start(bf16[8,2,256,256]{3,2,1,0:T(8,128)(2,1)} %shard_map.65), calls=%async_computation | async-start | bytes 4194304 | tf_op jit(solution)/shard_map/all_to_all | solution.py:549
  57.8 0.0 copy-done.2
  57.8 1.6 collective-permute-start
  59.4 0.0 copy-done.5
  59.4 0.1 constant_dynamic-slice_fusion
  59.6 0.6 collective-permute-start.3
  60.1 0.0 copy-done.3
  60.1 0.8 convert_reduce_fusion
  60.9 0.1 constant_dynamic-slice_fusion.2
  61.0 1.5 collective-permute-start.2
  62.6 0.1 copy.12
  62.7 3.9 %collective-permute-done.2 = s32[4,2,8]{1,2,0:T(8,128)S(1)} collective-permute-done((s32[4,2,8]{1,2,0:T(8,128)S(1)}, s32[4,2,8]{1,2,0:T(8,128)S(1)}, u32[]{:S(2)}, u32[]{:S(2)}) %collective-permute-start.2) | collective-permute-done | bytes 288 | tf_op jit(solution)/shard_map/ppermute | solution.py:16
  66.5 0.1 copy.13
  66.6 0.1 fusion.2
  66.7 0.1 lt.65
  66.8 0.0 collective-permute-done.3
  66.9 0.0 collective-permute-done
  66.9 0.0 copy-start.4
  66.9 0.7 copy-done.4
  67.6 1.2 maximum_select_fusion.q_ref
  68.8 36.3 %all-to-all-done.rows_ref = bf16[8,2,256,256]{3,2,1,0:T(8,128)(2,1)S(1)} async-done(((bf16[8,2,256,256]{3,2,1,0:T(8,128)(2,1)}), bf16[8,2,256,256]{3,2,1,0:T(8,128)(2,1)S(1)}, u32[]{:S(2)}, u32[]{:S(2)}) %all-to-all-start) | async-done | bytes 2097184 | tf_op jit(solution)/shard_map/all_to_all | solution.py:549
  105.1 10.2 %shard_map.66.heads_ref = bf16[128,2048]{1,0:T(8,128)(2,1)S(1)} custom-call(bf16[128,2048]{1,0:T(8,128)(2,1)S(1)} %maximum_select_fusion.q_ref, bf16[8,2,256,256]{3,2,1,0:T(8,128)(2,1)S(1)} %all-to-all-done.rows_ref, f32[2,1,2048]{2,1,0:T(1,128)S(1)} %compare_select_fusion.bias_ref, bf16[2,128,256]{2,1,0:T(8,128)(2,1)S(1)} %fusion.new_ref), custom_call_target="tpu_custom_call" | custom-call | tf_op jit(solution)/shard_map/pallas_call | solution.py:268
  115.3 59.9 %shard_map.67 = bf16[4,64,1024]{2,1,0:T(8,128)(2,1)S(1)} custom-call(s32[8]{0:T(128)S(1)} %copy-done, bf16[128,2048]{1,0:T(8,128)(2,1)S(1)} %shard_map.66.heads_ref, bf16[4096,1024]{1,0:T(8,128)(2,1)} %weight_hbm.1), custom_call_target="tpu_custom_call" | custom-call | tf_op jit(solution)/shard_map/pallas_call | solution.py:460
  175.3 0.8 copy.24
  (11 shorter events, 0.2 us)
Async XLA Ops:
  15.1 5.6 %copy-start = (s32[8]{0:T(128)S(1)}, s32[8]{0:T(128)}, u32[]{:S(2)}) copy-start(s32[8]{0:T(128)} %assign_ref.1) | copy-start | bytes 100
  17.8 26.1 %collective-permute-start.1 = (bf16[4,2,256,256]{3,2,1,0:T(8,128)(2,1)S(1)}, bf16[4,2,256,256]{3,2,1,0:T(8,128)(2,1)S(1)}, u32[]{:S(2)}, u32[]{:S(2)}) collective-permute-start(bf16[4,2,256,256]{3,2,1,0:T(8,128)(2,1)S(1)} %get-tuple-element.5), channel_id=1, source_target_pairs={{0,1},{1,0},{2,3},{3,2},{4,5},{5,4},{6,7},{7,6},{8,9},{9,8},{10,11... | collective-permute-start | bytes 3145736 | tf_op jit(solution)/shard_map/ppermute | solution.py:16
  43.9 1.0 copy-start.1
  51.6 6.2 %copy-start.2 = (bf16[1,64,4096]{2,1,0:T(8,128)(2,1)S(1)}, bf16[1,64,4096]{2,1,0:T(8,128)(2,1)}, u32[]{:S(2)}) copy-start(bf16[1,64,4096]{2,1,0:T(8,128)(2,1)} %param.9) | copy-start | bytes 1572868
  51.6 7.8 %copy-start.5 = (bf16[1,64,4,256]{3,2,1,0:T(4,128)(2,1)S(1)}, bf16[1,64,4,256]{3,2,1,0:T(4,128)(2,1)}, u32[]{:S(2)}) copy-start(bf16[1,64,4,256]{3,2,1,0:T(4,128)(2,1)} %param.10) | copy-start | bytes 393220
  51.6 8.6 %copy-start.3 = (s32[4,4,1024]{2,1,0:T(4,128)S(1)}, s32[4,4,1024]{2,1,0:T(4,128)}, u32[]{:S(2)}) copy-start(s32[4,4,1024]{2,1,0:T(4,128)} %param.7) | copy-start | bytes 196612
  51.6 53.5 %all-to-all-start = ((bf16[8,2,256,256]{3,2,1,0:T(8,128)(2,1)}), bf16[8,2,256,256]{3,2,1,0:T(8,128)(2,1)S(1)}, u32[]{:S(2)}, u32[]{:S(2)}) async-start(bf16[8,2,256,256]{3,2,1,0:T(8,128)(2,1)} %shard_map.65), calls=%async_computation | async-start | bytes 4194304 | tf_op jit(solution)/shard_map/all_to_all | solution.py:549
  57.8 9.1 %collective-permute-start = (bf16[64,2048]{1,0:T(8,128)(2,1)S(1)}, bf16[64,2048]{1,0:T(8,128)(2,1)S(1)}, u32[]{:S(2)}, u32[]{:S(2)}) collective-permute-start(bf16[64,2048]{1,0:T(8,128)(2,1)S(1)} %get-tuple-element.8), channel_id=1, source_target_pairs={{0,1},{1,0},{2,3},{3,2},{4,5},{5,4},{6,7},{7,6},{8,9},{9,8},{10,11... | collective-permute-start | bytes 786440 | tf_op jit(solution)/shard_map/ppermute | solution.py:16
  59.6 7.3 %collective-permute-start.3 = (bf16[64,2,256]{2,0,1:T(8,128)(2,1)S(1)}, bf16[64,2,256]{2,0,1:T(8,128)(2,1)S(1)}, u32[]{:S(2)}, u32[]{:S(2)}) collective-permute-start(bf16[64,2,256]{2,0,1:T(8,128)(2,1)S(1)} %bitcast.22), channel_id=1, source_target_pairs={{0,1},{1,0},{2,3},{3,2},{4,5},{5,4},{6,7},{7,6},{8,9},{9,8},{10,11... | collective-permute-start | bytes 196616 | tf_op jit(solution)/shard_map/ppermute | solution.py:16
  61.0 5.5 %collective-permute-start.2 = (s32[4,2,8]{1,2,0:T(8,128)S(1)}, s32[4,2,8]{1,2,0:T(8,128)S(1)}, u32[]{:S(2)}, u32[]{:S(2)}) collective-permute-start(s32[4,2,8]{1,2,0:T(8,128)S(1)} %get-tuple-element.12), channel_id=1, source_target_pairs={{0,1},{1,0},{2,3},{3,2},{4,5},{5,4},{6,7},{7,6},{8,9},{9,8},{10,11... | collective-permute-start | bytes 776 | tf_op jit(solution)/shard_map/ppermute | solution.py:16
  66.9 0.7 copy-start.4

commit v3 on v2

--- a/solution.py
+++ b/solution.py
@@ -163,70 +163,172 @@
     )
 
 
-def select_kernel(start_ref, kept_ref, cache_ref, out_ref):
+def places_kernel(start_ref, kept_ref, out_ref):
     start = start_ref[0]
-    kept = kept_ref[0]
-    total = kept.shape[1]
-    spots = cache_ref.shape[1]
-    capacity = out_ref.shape[1]
-    first = jnp.sum((kept < start).astype(jnp.int32))
-    wide = jnp.broadcast_to(kept, (8, total))
-    places = pltpu.roll(wide, lax.rem(total - first, total), 1)[:1, :capacity] - start
-    spot_ids = lax.broadcasted_iota(jnp.int32, (spots, capacity), 0)
-    chooser = (spot_ids == places).astype(jnp.float32).astype(jnp.bfloat16)
-    picked = lax.dot_general(
-        chooser, cache_ref[0], (((0,), (0,)), ((), ())), preferred_element_type=jnp.float32
-    )
-    out_ref[0] = picked.astype(out_ref.dtype)
-
-
-def select_rows(flat_cache, kept_lists, block_start, capacity):
+    lists, total = kept_ref.shape
+    capacity = out_ref.shape[2]
+    for i in range(lists):
+        kept = kept_ref[i : i + 1]
+        first = jnp.sum((kept < start).astype(jnp.int32))
+        wide = jnp.broadcast_to(kept, (8, total))
+        rolled = pltpu.roll(wide, lax.rem(total - first, total), 1)
+        out_ref[i] = rolled[:1, :capacity] - start
+
+
+def places_of(kept_lists, block_start, capacity):
+    return pl.pallas_call(
+        places_kernel,
+        out_shape=jax.ShapeDtypeStruct((kept_lists.shape[0], 1, capacity), jnp.int32),
+        in_specs=[
+            pl.BlockSpec(memory_space=pltpu.SMEM),
+            pl.BlockSpec(memory_space=pltpu.VMEM),
+        ],
+        out_specs=pl.BlockSpec(memory_space=pltpu.VMEM),
+    )(block_start.reshape(1), kept_lists)
+
+
+def relayout_kernel(
+    order_ref, places_ref, cache_hbm, out_ref,
+    cache, stage, outgoing, load_sem, y_send, y_recv, ctx_send, ctx_recv, *pool
+):
+    c = lax.axis_index("ctx")
+    d = lax.axis_index("dp")
+    groups = stage.shape[1]
+    slots = out_ref.shape[0]
+    kv_here = cache_hbm.shape[0] // groups
+    heads = kv_here // 2
+    capacity, width = places_ref.shape[2], cache.shape[2]
+    piece = stage.shape[2]
+    pieces = capacity // piece
+
+    def load(i):
+        return pltpu.make_async_copy(cache_hbm.at[i], cache.at[i], load_sem.at[i])
+
+    for j in range(heads):
+        for side in (1 - d, d):
+            for g in range(groups):
+                load(g * kv_here + side * heads + j).start()
+
+    barrier = pltpu.get_barrier_semaphore()
+    pl.semaphore_signal(barrier, inc=1, device_id={"dp": 1 - d}, device_id_type=MESH)
+    for k in range(1, slots):
+        pl.semaphore_signal(
+            barrier, inc=1, device_id={"ctx": lax.rem(c + k, slots)}, device_id_type=MESH
+        )
+    pl.semaphore_wait(barrier, slots)
+
+    spot_ids = lax.broadcasted_iota(jnp.int32, (cache.shape[1], capacity), 0)
+
+    def pick(i):
+        load(i).wait()
+        chooser = (spot_ids == places_ref[i]).astype(jnp.float32).astype(jnp.bfloat16)
+        return lax.dot_general(
+            chooser, cache[i], (((0,), (0,)), ((), ())), preferred_element_type=jnp.float32
+        ).astype(cache.dtype)
+
+    def y_copy(q, g, sender):
+        return pltpu.make_async_remote_copy(
+            src_ref=stage.at[q, g], dst_ref=pool[q].at[sender * groups + g], send_sem=y_send.at[q, g],
+            recv_sem=y_recv.at[q, g], device_id={"dp": 1 - d}, device_id_type=MESH,
+        )
+
+    def ctx_copy(q, k):
+        span = pl.ds((q % pieces) * piece, piece)
+        return pltpu.make_async_remote_copy(
+            src_ref=outgoing.at[q, k - 1], dst_ref=out_ref.at[c, q // pieces, span],
+            send_sem=ctx_send.at[q, k - 1], recv_sem=ctx_recv.at[q, k - 1],
+            device_id={"ctx": lax.rem(c + k, slots)}, device_id_type=MESH,
+        )
+
+    def pick_theirs(j):
+        def step(g, carry):
+            picked = pick(g * kv_here + (1 - d) * heads + j)
+            for half in range(pieces):
+                stage[j * pieces + half, g] = picked[half * piece : (half + 1) * piece]
+            y_copy(j * pieces, g, d).start()
+            return carry
+
+        lax.fori_loop(0, groups, step, 0)
+        for half in range(1, pieces):
+            for g in range(groups):
+                y_copy(j * pieces + half, g, d).start()
+
+    def pick_mine(j):
+        def step(g, carry):
+            picked = pick(g * kv_here + d * heads + j)
+            for half in range(pieces):
+                pool[j * pieces + half][d * groups + g] = picked[half * piece : (half + 1) * piece]
+            return carry
+
+        lax.fori_loop(0, groups, step, 0)
+
+    def scatter(q):
+        for g in range(groups):
+            y_copy(q, g, 1 - d).wait_recv()
+        for k in (4, 5, 3, 2, 6, 1, 7) if slots == 8 else range(1, slots):
+            outgoing[q, k - 1] = pool[q][order_ref[lax.rem(c + k, slots)]]
+            ctx_copy(q, k).start()
+        start = (q % pieces) * piece
+        out_ref[c, q // pieces, start : start + piece] = pool[q][order_ref[c]]
+
+    pick_theirs(0)
+    pick_mine(0)
+    for j in range(heads):
+        if j + 1 < heads:
+            pick_theirs(j + 1)
+        for half in range(pieces):
+            scatter(j * pieces + half)
+            if half == 0 and j + 1 < heads:
+                pick_mine(j + 1)
+
+    for q in range(heads * pieces):
+        for k in range(1, slots):
+            sender = lax.rem(c + slots - k, slots)
+            start = (q % pieces) * piece
+            pltpu.make_async_remote_copy(
+                src_ref=outgoing.at[q, k - 1],
+                dst_ref=out_ref.at[sender, q // pieces, pl.ds(start, piece)],
+                send_sem=ctx_send.at[q, k - 1], recv_sem=ctx_recv.at[q, k - 1],
+                device_id={"ctx": lax.rem(c + k, slots)}, device_id_type=MESH,
+            ).wait()
+        for g in range(groups):
+            y_copy(q, g, d).wait_send()
+
+
+def relayout(flat_cache, places, order, groups):
     lists, spots, width = flat_cache.shape
-    total = kept_lists.shape[1]
+    capacity = places.shape[2]
+    slots = order.shape[0]
+    heads = lists // groups // 2
+    pieces = 2
+    piece = capacity // pieces
+    kind = flat_cache.dtype
+    dma = pltpu.SemaphoreType.DMA
     return pl.pallas_call(
-        select_kernel,
-        out_shape=jax.ShapeDtypeStruct((lists, capacity, width), flat_cache.dtype),
-        grid_spec=pltpu.PrefetchScalarGridSpec(
-            num_scalar_prefetch=1,
-            grid=(lists,),
-            in_specs=[
-                pl.BlockSpec((1, 1, total), lambda i, s: (i, 0, 0)),
-                pl.BlockSpec((1, spots, width), lambda i, s: (i, 0, 0)),
-            ],
-            out_specs=pl.BlockSpec((1, capacity, width), lambda i, s: (i, 0, 0)),
+        relayout_kernel,
+        out_shape=jax.ShapeDtypeStruct((slots, heads, capacity, width), kind),
+        in_specs=[
+            pl.BlockSpec(memory_space=pltpu.SMEM),
+            pl.BlockSpec(memory_space=pltpu.VMEM),
+            pl.BlockSpec(memory_space=pl.ANY),
+        ],
+        out_specs=pl.BlockSpec(memory_space=pltpu.VMEM),
+        scratch_shapes=[
+            pltpu.VMEM((lists, spots, width), kind),
+            pltpu.VMEM((heads * pieces, groups, piece, width), kind),
+            pltpu.VMEM((heads * pieces, slots - 1, piece, width), kind),
+            dma((lists,)),
+            dma((heads * pieces, groups)),
+            dma((heads * pieces, groups)),
+            dma((heads * pieces, slots - 1)),
+            dma((heads * pieces, slots - 1)),
+        ]
+        + [pltpu.VMEM((2 * groups, piece, width), kind)] * (heads * pieces),
+        cost_estimate=pl.CostEstimate(flops=int(3e10), bytes_accessed=int(1.5e8), transcendentals=0),
+        compiler_params=pltpu.CompilerParams(
+            collective_id=0, has_side_effects=True, vmem_limit_bytes=48 * 1024 * 1024
         ),
-    )(block_start.reshape(1), kept_lists.reshape(lists, 1, total), flat_cache)
-
-
-def arrange_kernel(groups, order_ref, dp_ref, mine_ref, got_ref, out_ref):
-    from_mine = order_ref[pl.program_id(0)] // groups == dp_ref[0]
-
-    @pl.when(from_mine)
-    def _():
-        out_ref[...] = mine_ref[...]
-
-    @pl.when(jnp.logical_not(from_mine))
-    def _():
-        out_ref[...] = got_ref[...]
-
-
-def arrange(mine, got, order, dp_id):
-    groups, heads, capacity, width = mine.shape
-    block = (1, heads, capacity, width)
-
-    def source(i, order_ref, dp_ref):
-        return (order_ref[i] % groups, 0, 0, 0)
-
-    return pl.pallas_call(
-        functools.partial(arrange_kernel, groups),
-        out_shape=jax.ShapeDtypeStruct((order.shape[0], heads, capacity, width), mine.dtype),
-        grid_spec=pltpu.PrefetchScalarGridSpec(
-            num_scalar_prefetch=2,
-            grid=(order.shape[0],),
-            in_specs=[pl.BlockSpec(block, source), pl.BlockSpec(block, source)],
-            out_specs=pl.BlockSpec(block, lambda i, a, b: (i, 0, 0, 0)),
-        ),
-    )(order, dp_id.reshape(1), mine, got)
+    )(order, places, flat_cache)
 
 
 def attend_kernel(q_ref, rows_ref, bias_ref, new_ref, out_ref):
@@ -533,20 +635,14 @@
     if kv_here % 2 or lax.axis_size("ctx") != 8 or lax.axis_size("tensor") != 2:
         return local_by_rows(cache, kept, assign, queries, new_kv, out_weight)
     ctx_id = lax.axis_index("ctx")
-    dp_id = lax.axis_index("dp")
     capacity = ctx_dev // 2
     per_group = queries.shape[2] // (kv_here * (width // 2))
     order, query, new_rows, bias = prepare(cache, kept, assign, queries, new_kv)
-    picked = select_rows(
-        cache.reshape(groups * kv_here, ctx_dev, width),
-        kept.reshape(groups * kv_here, kept.shape[2]),
-        ctx_id * ctx_dev,
-        capacity,
-    ).reshape(groups, kv_here, capacity, width)
-    picked_mine, picked_theirs = halves_of(picked, dp_id, 1)
-    picked_got = swapped(picked_theirs, "dp", 0)
-    buffer = arrange(picked_mine, picked_got, order, dp_id)
-    received = lax.all_to_all(buffer, "ctx", split_axis=0, concat_axis=0, tiled=True)
+    places = places_of(
+        kept.reshape(groups * kv_here, kept.shape[2]), ctx_id * ctx_dev, capacity
+    )
+    flat_cache = cache.reshape(groups * kv_here, ctx_dev, width)
+    received = relayout(flat_cache, places, order, groups)
     head_out = attend_heads(query, received, bias, new_rows, per_group)
     return gather_project(head_out, out_weight, assign)
 

time: 177 us -> 146 us (0.82)
  waiting for transfers between devices: 62.7 us -> 0.01 us
  Pallas kernels: 90.4 us -> 132 us
  starting transfers between devices: 12.8 us -> 5.13 us
    pallas_call x2, Pallas kernels: 20.2 us -> 58.7 us  [the longest x1 55.8 us: relayout(): pl.pallas_call(relayout_kernel, out_shape=jax.ShapeDtypeStruct((slots, he...]
    all_to_all x1 -> x0, waiting for transfers between devices: 36.3 us -> none  [local(): lax.all_to_all(buffer, 'ctx', split_axis=0, concat_axis=0, tiled=True)]
    ppermute x4 -> x3, waiting for transfers between devices: 26.4 us -> 0.01 us  [swapped(): lax.ppermute(array, axis, [(i, i ^ 1 << distance) for i in range(lax.axis...]
    all_to_all x1 -> x0, starting transfers between devices: 6.17 us -> none  [local(): lax.all_to_all(buffer, 'ctx', split_axis=0, concat_axis=0, tiled=True)]
    pallas_call x1, Pallas kernels: 59.9 us -> 63.1 us  [gather_project(): pl.pallas_call(gather_project_kernel, out_shape=jax.ShapeDtypeStruct((kep...]
    dynamic_slice x2 -> x1, local copies, waits for them, and re-layouts: 2.69 us -> 0.01 us  [halves_of(): theirs = lax.dynamic_slice_in_dim(array, (1 - dp_id) * size, size, axis)]
    dynamic_slice x5, local copies, waits for them, and re-layouts: 0.37 us -> 2.37 us  [halves_of(): mine = lax.dynamic_slice_in_dim(array, dp_id * size, size, axis)]
    ppermute x4 -> x3, starting transfers between devices: 6.65 us -> 5.13 us  [swapped(): lax.ppermute(array, axis, [(i, i ^ 1 << distance) for i in range(lax.axis...]
  transfers between devices with their start and end apart: 5 -> 3, of which waited for: 3 -> 0; matrix products, arithmetic and copies ran while one was open for 2% -> 4% of each run, Pallas kernels for 0% -> 40%
where the time goes in v3:
time: 146 us
  Pallas kernels  132 us (90%)
  local copies, waits for them, and re-layouts  5.59 us (4%)
  starting transfers between devices  5.13 us (4%)
  other arithmetic  3.28 us (2%)
    pallas_call x1, Pallas kernels, gather_project(): pl.pallas_call(gather_project_kernel, out_shape=jax.ShapeDtypeStruct((kep...  63.1 us
    pallas_call x1, Pallas kernels, relayout(): pl.pallas_call(relayout_kernel, out_shape=jax.ShapeDtypeStruct((slots, he...  55.8 us
    pallas_call x1, Pallas kernels, attend_heads(): pl.pallas_call(attend_kernel, out_shape=jax.ShapeDtypeStruct(query.shape,...  10.2 us
    ppermute x3, starting transfers between devices, swapped(): lax.ppermute(array, axis, [(i, i ^ 1 << distance) for i in range(lax.axis...  5.13 us
  transfers between devices with their start and end apart: 3, of which 0 were waited for; matrix products, arithmetic and copies ran while one was open for 4% of the time, Pallas kernels for 40%

profile of v3, /device:TPU:0, one launch (start us, length us, event | category | flops | bytes accessed | tf_op | source)
XLA Modules:
  0.0 146.1 jit_solution(11659186322567101738)
XLA Ops:
  0.0 1.6 %convert_reduce_fusion = s32[4,4,9]{1,2,0:T(8,128)S(1)} fusion(s32[4,4,1024]{2,1,0:T(4,128)} %param.7, s32[9]{0:T(128)S(1)} %iota_multiply_fusion), kind=kLoop, calls=%fused_computation | loop fusion | flops 442224 | bytes 66148 | tf_op jit(solution)/shard_map/reduce_sum | solution.py:615
  1.6 0.1 constant_dynamic-slice_fusion.2
  1.7 3.0 %collective-permute-start.1 = (s32[4,2,8]{1,2,0:T(8,128)S(1)}, s32[4,2,8]{1,2,0:T(8,128)S(1)}, u32[]{:S(2)}, u32[]{:S(2)}) collective-permute-start(s32[4,2,8]{1,2,0:T(8,128)S(1)} %get-tuple-element.10), channel_id=1, source_target_pairs={{0,1},{1,0},{2,3},{3,2},{4,5},{5,4},{6,7},{7,6},{8,9},{9,8},{10,11... | collective-permute-start | bytes 776 | tf_op jit(solution)/shard_map/ppermute | solution.py:16
  4.7 1.1 constant_dynamic-slice_fusion
  5.8 0.1 collective-permute-start.2
  5.9 1.1 dynamic-slice_bitcast_fusion.1
  7.0 2.1 %collective-permute-start = (bf16[64,2048]{1,0:T(8,128)(2,1)S(1)}, bf16[64,2048]{1,0:T(8,128)(2,1)S(1)}, u32[]{:S(2)}, u32[]{:S(2)}) collective-permute-start(bf16[64,2048]{1,0:T(8,128)(2,1)S(1)} %get-tuple-element.6), channel_id=1, source_target_pairs={{0,1},{1,0},{2,3},{3,2},{4,5},{5,4},{6,7},{7,6},{8,9},{9,8},{10,11... | collective-permute-start | bytes 786440 | tf_op jit(solution)/shard_map/ppermute | solution.py:16
  9.1 1.5 %reshape.60.kept_ref = s32[16,1024]{1,0:T(8,128)} reshape(s32[4,4,1024]{2,1,0:T(4,128)} %param.7) | data formatting | bytes 131072 | tf_op jit(solution)/shard_map/reshape | solution.py:642
  10.5 0.8 select_reduce_fusion.order_ref
  11.3 0.7 compare_convert_fusion
  12.0 2.9 %shard_map.64.places_ref = s32[16,1,256]{2,1,0:T(1,128)} custom-call(s32[1]{0:T(128)} %bitcast.2.start_ref, s32[16,1024]{1,0:T(8,128)} %reshape.60.kept_ref), custom_call_target="tpu_custom_call" | custom-call | tf_op jit(solution)/shard_map/pallas_call | solution.py:179
  14.8 0.0 copy-start
  14.9 0.7 copy-done
  15.6 55.8 %shard_map.65.rows_ref = bf16[8,2,256,256]{3,2,1,0:T(8,128)(2,1)S(1)} custom-call(s32[8]{0:T(128)S(1)} %select_reduce_fusion.order_ref, s32[16,1,256]{2,1,0:T(1,128)S(1)} %copy-done, bf16[16,512,256]{2,1,0:T(8,128)(2,1)} %bitcast.20), custom_call_target="tpu_custom_call" | custom-call | flops 30000001024 | bytes 150000000 | tf_op jit(solution)/shard_map/pallas_call | solution.py:307
  71.4 0.0 copy-start.1
  71.4 0.1 copy.12
  71.5 0.0 collective-permute-done.1
  71.5 0.1 copy.13
  71.6 0.1 fusion.2
  71.7 0.1 lt.63
  71.9 0.0 collective-permute-done.2
  71.9 0.0 collective-permute-done
  71.9 0.1 maximum_select_fusion.q_ref
  72.0 10.2 %shard_map.66.heads_ref = bf16[128,2048]{1,0:T(8,128)(2,1)S(1)} custom-call(bf16[128,2048]{1,0:T(8,128)(2,1)S(1)} %maximum_select_fusion.q_ref, bf16[8,2,256,256]{3,2,1,0:T(8,128)(2,1)S(1)} %shard_map.65.rows_ref, f32[2,1,2048]{2,1,0:T(1,128)S(1)} %compare_select_fusion.bias_ref, bf16[2,128,256]{2,1,0:T(8,128)(2,1)S(1)} %fusion.new_ref), custom_call_target="tpu_custom_call" | custom-call | tf_op jit(solution)/shard_map/pallas_call | solution.py:370
  82.2 0.0 copy-done.1
  82.2 63.1 %shard_map.67 = bf16[4,64,1024]{2,1,0:T(8,128)(2,1)S(1)} custom-call(s32[8]{0:T(128)S(1)} %copy-done.1, bf16[128,2048]{1,0:T(8,128)(2,1)S(1)} %shard_map.66.heads_ref, bf16[4096,1024]{1,0:T(8,128)(2,1)} %weight_hbm.1), custom_call_target="tpu_custom_call" | custom-call | tf_op jit(solution)/shard_map/pallas_call | solution.py:562
  145.3 0.8 copy.24
  (9 shorter events, 0.1 us)
Async XLA Ops:
  1.7 69.8 %collective-permute-start.1 = (s32[4,2,8]{1,2,0:T(8,128)S(1)}, s32[4,2,8]{1,2,0:T(8,128)S(1)}, u32[]{:S(2)}, u32[]{:S(2)}) collective-permute-start(s32[4,2,8]{1,2,0:T(8,128)S(1)} %get-tuple-element.10), channel_id=1, source_target_pairs={{0,1},{1,0},{2,3},{3,2},{4,5},{5,4},{6,7},{7,6},{8,9},{9,8},{10,11... | collective-permute-start | bytes 776 | tf_op jit(solution)/shard_map/ppermute | solution.py:16
  5.8 66.0 %collective-permute-start.2 = (bf16[64,2,256]{2,0,1:T(8,128)(2,1)S(1)}, bf16[64,2,256]{2,0,1:T(8,128)(2,1)S(1)}, u32[]{:S(2)}, u32[]{:S(2)}) collective-permute-start(bf16[64,2,256]{2,0,1:T(8,128)(2,1)S(1)} %bitcast.18), channel_id=1, source_target_pairs={{0,1},{1,0},{2,3},{3,2},{4,5},{5,4},{6,7},{7,6},{8,9},{9,8},{10,11... | collective-permute-start | bytes 196616 | tf_op jit(solution)/shard_map/ppermute | solution.py:16
  7.0 64.9 %collective-permute-start = (bf16[64,2048]{1,0:T(8,128)(2,1)S(1)}, bf16[64,2048]{1,0:T(8,128)(2,1)S(1)}, u32[]{:S(2)}, u32[]{:S(2)}) collective-permute-start(bf16[64,2048]{1,0:T(8,128)(2,1)S(1)} %get-tuple-element.6), channel_id=1, source_target_pairs={{0,1},{1,0},{2,3},{3,2},{4,5},{5,4},{6,7},{7,6},{8,9},{9,8},{10,11... | collective-permute-start | bytes 786440 | tf_op jit(solution)/shard_map/ppermute | solution.py:16
  14.8 0.7 copy-start
  71.4 10.8 %copy-start.1 = (s32[8]{0:T(128)S(1)}, s32[8]{0:T(128)}, u32[]{:S(2)}) copy-start(s32[8]{0:T(128)} %assign_ref.1) | copy-start | bytes 100

commit v4 on v3

--- a/solution.py
+++ b/solution.py
@@ -188,8 +188,9 @@
 
 
 def relayout_kernel(
-    order_ref, places_ref, cache_hbm, out_ref,
-    cache, stage, outgoing, load_sem, y_send, y_recv, ctx_send, ctx_recv, *pool
+    order_ref, places_ref, cache_hbm, query_hbm, new_hbm, bias_hbm, head_out_ref,
+    out_ref, query, new_rows, bias, cache, stage, outgoing,
+    load_sem, y_send, y_recv, ctx_send, ctx_recv, side_send, side_recv, side_own, *pool
 ):
     c = lax.axis_index("ctx")
     d = lax.axis_index("dp")
@@ -217,6 +218,33 @@
         )
     pl.semaphore_wait(barrier, slots)
 
+    rows, columns = query_hbm.shape[0], query.shape[1]
+
+    def side_parts(side, place):
+        across = pl.ds(pl.multiple_of(side * columns, columns), columns)
+        down = pl.ds(pl.multiple_of(place * rows, rows), rows)
+        return (
+            (query_hbm.at[:, across], query.at[down]),
+            (new_hbm.at[side], new_rows.at[:, down]),
+            (bias_hbm.at[side], bias.at[pl.ds(place * groups, groups)]),
+        )
+
+    def side_sends(place):
+        return [
+            pltpu.make_async_remote_copy(
+                src_ref=source, dst_ref=target, send_sem=side_send.at[i], recv_sem=side_recv.at[i],
+                device_id={"dp": 1 - d}, device_id_type=MESH,
+            )
+            for i, (source, target) in enumerate(side_parts(1 - d, place))
+        ]
+
+    own_parts = [
+        pltpu.make_async_copy(source, target, side_own.at[i])
+        for i, (source, target) in enumerate(side_parts(d, d))
+    ]
+    for part in own_parts:
+        part.start()
+
     spot_ids = lax.broadcasted_iota(jnp.int32, (cache.shape[1], capacity), 0)
 
     def pick(i):
@@ -280,8 +308,11 @@
             scatter(j * pieces + half)
             if half == 0 and j + 1 < heads:
                 pick_mine(j + 1)
-
-    for q in range(heads * pieces):
+            if half == 0 and j == 0:
+                for part in side_sends(d):
+                    part.start()
+
+    def finish(q):
         for k in range(1, slots):
             sender = lax.rem(c + slots - k, slots)
             start = (q % pieces) * piece
@@ -294,8 +325,33 @@
         for g in range(groups):
             y_copy(q, g, d).wait_send()
 
-
-def relayout(flat_cache, places, order, groups):
+    hd = width // 2
+    tiles = columns // heads // (2 * hd)
+    for h in range(heads):
+        for half in range(pieces):
+            finish(h * pieces + half)
+        if h == 0:
+            for part in own_parts:
+                part.wait()
+            for part in side_sends(1 - d):
+                part.wait_recv()
+
+        def tile_step(n, carry):
+            low = pl.multiple_of((h * tiles + n) * 2 * hd, 2 * hd)
+            first, second = attend_tile(
+                query[:, pl.ds(low, hd)], query[:, pl.ds(low + hd, hd)],
+                out_ref[:, h], bias[order_ref[c], h : h + 1], new_rows[h],
+            )
+            head_out_ref[:, pl.ds(low, hd)] = first
+            head_out_ref[:, pl.ds(low + hd, hd)] = second
+            return carry
+
+        lax.fori_loop(0, tiles, tile_step, 0)
+    for part in side_sends(d):
+        part.wait_send()
+
+
+def relayout_attend(flat_cache, places, order, groups, queries, new_sides, bias_sides):
     lists, spots, width = flat_cache.shape
     capacity = places.shape[2]
     slots = order.shape[0]
@@ -303,17 +359,25 @@
     pieces = 2
     piece = capacity // pieces
     kind = flat_cache.dtype
+    rows, columns = queries.shape[0], queries.shape[1] // 2
     dma = pltpu.SemaphoreType.DMA
     return pl.pallas_call(
         relayout_kernel,
-        out_shape=jax.ShapeDtypeStruct((slots, heads, capacity, width), kind),
+        out_shape=jax.ShapeDtypeStruct((2 * rows, columns), kind),
         in_specs=[
             pl.BlockSpec(memory_space=pltpu.SMEM),
             pl.BlockSpec(memory_space=pltpu.VMEM),
             pl.BlockSpec(memory_space=pl.ANY),
+            pl.BlockSpec(memory_space=pl.ANY),
+            pl.BlockSpec(memory_space=pltpu.VMEM),
+            pl.BlockSpec(memory_space=pltpu.VMEM),
         ],
         out_specs=pl.BlockSpec(memory_space=pltpu.VMEM),
         scratch_shapes=[
+            pltpu.VMEM((slots, heads, capacity, width), kind),
+            pltpu.VMEM((2 * rows, columns), kind),
+            pltpu.VMEM((heads, 2 * rows, width), kind),
+            pltpu.VMEM((2 * groups,) + bias_sides.shape[2:], jnp.float32),
             pltpu.VMEM((lists, spots, width), kind),
             pltpu.VMEM((heads * pieces, groups, piece, width), kind),
             pltpu.VMEM((heads * pieces, slots - 1, piece, width), kind),
@@ -322,28 +386,30 @@
             dma((heads * pieces, groups)),
             dma((heads * pieces, slots - 1)),
             dma((heads * pieces, slots - 1)),
+            dma((3,)),
+            dma((3,)),
+            dma((3,)),
         ]
         + [pltpu.VMEM((2 * groups, piece, width), kind)] * (heads * pieces),
         cost_estimate=pl.CostEstimate(flops=int(3e10), bytes_accessed=int(1.5e8), transcendentals=0),
         compiler_params=pltpu.CompilerParams(
             collective_id=0, has_side_effects=True, vmem_limit_bytes=48 * 1024 * 1024
         ),
-    )(order, places, flat_cache)
-
-
-def attend_kernel(q_ref, rows_ref, bias_ref, new_ref, out_ref):
-    blocks, _, capacity, width = rows_ref.shape
-    hd = width // 2
-    rows = q_ref.shape[0]
-    q = jnp.concatenate([q_ref[:, :hd], q_ref[:, hd:]], axis=0)
-    keys = rows_ref[:, 0, :, :hd].reshape(blocks * capacity, hd)
-    values = rows_ref[:, 0, :, hd:].reshape(blocks * capacity, hd)
-    new_keys = new_ref[0, :, :hd]
-    new_values = new_ref[0, :, hd:]
+    )(order, places, flat_cache, queries, new_sides, bias_sides)
+
+
+def attend_tile(first_query, second_query, received, bias, new_rows):
+    blocks, capacity, width = received.shape
+    rows, hd = first_query.shape
+    q = jnp.concatenate([first_query, second_query], axis=0)
+    keys = received[:, :, :hd].reshape(blocks * capacity, hd)
+    values = received[:, :, hd:].reshape(blocks * capacity, hd)
+    new_keys = new_rows[:, :hd]
+    new_values = new_rows[:, hd:]
     scale = hd**-0.5 * math.log2(math.e)
     dims = (((1,), (1,)), ((), ()))
     kept_scores = lax.dot_general(q, keys, dims, preferred_element_type=jnp.float32) * scale
-    kept_scores = kept_scores + bias_ref[0]
+    kept_scores = kept_scores + bias
     new_scores = lax.dot_general(q, new_keys, dims, preferred_element_type=jnp.float32) * scale
     row_ids = lax.rem(lax.broadcasted_iota(jnp.int32, new_scores.shape, 0), rows)
     key_ids = lax.broadcasted_iota(jnp.int32, new_scores.shape, 1)
@@ -357,29 +423,8 @@
     weighted = jnp.dot(
         kept_weights.astype(jnp.bfloat16), values, preferred_element_type=jnp.float32
     ) + jnp.dot(new_weights.astype(jnp.bfloat16), new_values, preferred_element_type=jnp.float32)
-    result = (weighted / total).astype(out_ref.dtype)
-    out_ref[:, :hd] = result[:rows]
-    out_ref[:, hd:] = result[rows:]
-
-
-def attend_heads(query, received, bias, new_rows, per_group):
-    rows, columns = query.shape
-    blocks, heads, capacity, width = received.shape
-    hd = width // 2
-    pairs = per_group // 2
-    return pl.pallas_call(
-        attend_kernel,
-        out_shape=jax.ShapeDtypeStruct(query.shape, query.dtype),
-        grid=(heads, pairs),
-        in_specs=[
-            pl.BlockSpec((rows, 2 * hd), lambda h, j: (0, h * pairs + j)),
-            pl.BlockSpec((blocks, 1, capacity, width), lambda h, j: (0, h, 0, 0)),
-            pl.BlockSpec((1, 1, blocks * capacity), lambda h, j: (h, 0, 0)),
-            pl.BlockSpec((1, rows, width), lambda h, j: (h, 0, 0)),
-        ],
-        out_specs=pl.BlockSpec((rows, 2 * hd), lambda h, j: (0, h * pairs + j)),
-        compiler_params=pltpu.CompilerParams(vmem_limit_bytes=48 * 1024 * 1024),
-    )(query, received, bias, new_rows)
+    result = (weighted / total).astype(first_query.dtype)
+    return result[:rows], result[rows:]
 
 
 def gather_project_kernel(
@@ -413,10 +458,14 @@
 
     pl.semaphore_wait(barrier, 3 + (z > 0).astype(jnp.int32) + (z < zs - 1).astype(jnp.int32))
 
-    cols = (d, 1 - d)
+    cut = rows // 4
+    spans = ((d, 0, cut), (d, cut, rows), (1 - d, 0, rows // 2), (1 - d, rows // 2, rows))
+    x_first = (0,)
+    z_first = (1, 2, 3)
 
     def copy(piece, slot, channel):
-        ref = gat.at[cols[piece], slot]
+        col, low, high = spans[piece]
+        ref = gat.at[col, slot, pl.ds(low, high - low)]
         target = (c + 2, c - 2, partner_x)[channel]
         return pltpu.make_async_remote_copy(
             src_ref=ref, dst_ref=ref, send_sem=send.at[piece, slot, channel],
@@ -436,48 +485,52 @@
     def arrived(piece, slot):
         copy(piece, slot, 2).wait_recv()
 
-    y_copy = pltpu.make_async_remote_copy(
-        src_ref=heads_ref.at[pl.ds((1 - d) * rows, rows)], dst_ref=gat.at[d, c],
-        send_sem=y_send, recv_sem=recv.at[1, c], device_id={"dp": 1 - d}, device_id_type=MESH,
-    )
-    y_copy.start()
+    def y_copy(piece):
+        _, low, high = spans[piece]
+        return pltpu.make_async_remote_copy(
+            src_ref=heads_ref.at[pl.ds(pl.multiple_of((1 - d) * rows + low, 16), high - low)],
+            dst_ref=gat.at[d, c, pl.ds(low, high - low)],
+            send_sem=y_send.at[piece - 2], recv_sem=recv.at[piece, c],
+            device_id={"dp": 1 - d}, device_id_type=MESH,
+        )
+
+    y_copy(2).start()
+    y_copy(3).start()
     gat[d, c] = heads_ref[pl.ds(pl.multiple_of(d * rows, rows), rows)]
+    copy(0, c, 2).start()
+    up(1, c)
+    down(1, c)
+    copy(1, c, 2).start()
     up(0, c)
     down(0, c)
-    copy(0, c, 2).start()
-    arrived(1, c)
-    copy(1, c, 2).start()
-    up(1, c)
-    down(1, c)
-    arrived(1, partner_x)
-    up(1, partner_x)
-    down(1, partner_x)
+    for piece in (2, 3):
+        arrived(piece, c)
+        up(piece, c)
+        down(piece, c)
+        copy(piece, c, 2).start()
+    arrived(0, partner_x)
+    up(0, partner_x)
+    down(0, partner_x)
     for k in range(1, zs):
-        @pl.when(z >= k)
-        def _():
-            arrived(0, c - 2 * k)
-            up(0, c - 2 * k)
-            copy(0, c - 2 * k, 2).start()
-
-        @pl.when(z + k < zs)
-        def _():
-            arrived(0, c + 2 * k)
-            down(0, c + 2 * k)
-            copy(0, c + 2 * k, 2).start()
-
-        for base in (c, partner_x):
-            @pl.when(z >= k)
-            def _():
-                arrived(1, base - 2 * k)
-                up(1, base - 2 * k)
-
-            @pl.when(z + k < zs)
-            def _():
-                arrived(1, base + 2 * k)
-                down(1, base + 2 * k)
-
-    for zo in range(zs):
-        arrived(0, zo * 2 + 1 - x)
+        for piece in (1, 0, 2, 3):
+            for base in (c, partner_x) if piece in x_first else (c,):
+                @pl.when(z >= k)
+                def _():
+                    arrived(piece, base - 2 * k)
+                    up(piece, base - 2 * k)
+                    if piece in z_first:
+                        copy(piece, base - 2 * k, 2).start()
+
+                @pl.when(z + k < zs)
+                def _():
+                    arrived(piece, base + 2 * k)
+                    down(piece, base + 2 * k)
+                    if piece in z_first:
+                        copy(piece, base + 2 * k, 2).start()
+
+    for piece in z_first:
+        for zo in range(zs):
+            arrived(piece, zo * 2 + 1 - x)
     load_weight.wait()
 
     slots = gat.shape[1]
@@ -510,44 +563,39 @@
             total = part[n, assign_ref[t * kept + j]] + recv_buf[n, j].astype(jnp.float32)
             out_ref[j, :, n * tile : (n + 1) * tile] = total.astype(out_ref.dtype)
 
-    y_copy.wait_send()
+    y_copy(2).wait_send()
+    y_copy(3).wait_send()
     for n in range(tiles):
         exchange(n).wait_send()
-    copy(0, c, 2).wait_send()
-    copy(1, c, 2).wait_send()
-
-    @pl.when(z < zs - 1)
-    def _():
-        copy(0, c, 0).wait_send()
-        copy(1, c, 0).wait_send()
-        copy(1, partner_x, 0).wait_send()
-
-    @pl.when(z > 0)
-    def _():
-        copy(0, c, 1).wait_send()
-        copy(1, c, 1).wait_send()
-        copy(1, partner_x, 1).wait_send()
-
-    for k in range(1, zs):
-        @pl.when(z >= k)
-        def _():
-            copy(0, c - 2 * k, 2).wait_send()
-
+    for piece in x_first + z_first:
+        copy(piece, c, 2).wait_send()
+        for base in (c, partner_x) if piece in x_first else (c,):
             @pl.when(z < zs - 1)
             def _():
-                copy(0, c - 2 * k, 0).wait_send()
-                copy(1, c - 2 * k, 0).wait_send()
-                copy(1, partner_x - 2 * k, 0).wait_send()
-
-        @pl.when(z + k < zs)
-        def _():
-            copy(0, c + 2 * k, 2).wait_send()
+                copy(piece, base, 0).wait_send()
 
             @pl.when(z > 0)
             def _():
-                copy(0, c + 2 * k, 1).wait_send()
-                copy(1, c + 2 * k, 1).wait_send()
-                copy(1, partner_x + 2 * k, 1).wait_send()
+                copy(piece, base, 1).wait_send()
+
+            for k in range(1, zs):
+                @pl.when(z >= k)
+                def _():
+                    if piece in z_first:
+                        copy(piece, base - 2 * k, 2).wait_send()
+
+                    @pl.when(z < zs - 1)
+                    def _():
+                        copy(piece, base - 2 * k, 0).wait_send()
+
+                @pl.when(z + k < zs)
+                def _():
+                    if piece in z_first:
+                        copy(piece, base + 2 * k, 2).wait_send()
+
+                    @pl.when(z > 0)
+                    def _():
+                        copy(piece, base + 2 * k, 1).wait_send()
 
 
 def gather_project(head_out, out_weight, assign):
@@ -574,9 +622,9 @@
             pltpu.VMEM((tiles, slots, rows, tile), jnp.float32),
             pltpu.VMEM((tiles, kept, rows, tile), kind),
             pltpu.VMEM((tiles, kept, rows, tile), kind),
-            dma((2, slots, 3)),
-            dma((2, slots)),
-            dma,
+            dma((4, slots, 3)),
+            dma((4, slots)),
+            dma((2,)),
             dma((tiles,)),
             dma((tiles,)),
             dma,
@@ -587,63 +635,30 @@
     )(assign, head_out, out_weight)
 
 
-def in_dp_order(own, other, dp_id, axis):
-    return jnp.where(
-        dp_id == 0,
-        jnp.concatenate([own, other], axis=axis),
-        jnp.concatenate([other, own], axis=axis),
-    )
-
-
-def halves_of(array, dp_id, axis):
-    size = array.shape[axis] // 2
-    mine = lax.dynamic_slice_in_dim(array, dp_id * size, size, axis)
-    theirs = lax.dynamic_slice_in_dim(array, (1 - dp_id) * size, size, axis)
-    return mine, theirs
-
-
-def prepare(cache, kept, assign, queries, new_kv):
+def local(cache, kept, assign, queries, new_kv, out_weight):
+    groups, kv_here, ctx_dev, width = cache.shape
     ctx_count = lax.axis_size("ctx")
+    if kv_here % 2 or ctx_count != 8 or lax.axis_size("tensor") != 2:
+        return local_by_rows(cache, kept, assign, queries, new_kv, out_weight)
     ctx_id = lax.axis_index("ctx")
-    dp_id = lax.axis_index("dp")
-    groups, kv_here, ctx_dev, width = cache.shape
-    total = kept.shape[2]
-    prompts = assign.shape[0]
-    slots = jnp.arange(prompts, dtype=jnp.int32)
+    capacity = ctx_dev // 2
+    heads = kv_here // 2
+    rows = queries.shape[1]
+    slots = jnp.arange(assign.shape[0], dtype=jnp.int32)
     order = jnp.sum(jnp.where(assign[None, :] == slots[:, None], slots[None, :], 0), axis=1)
     edges = ctx_dev * jnp.arange(ctx_count + 1, dtype=jnp.int32)
     below = jnp.sum((kept[:, :, None, :] < edges[:, None]).astype(jnp.int32), axis=3)
     counts = below[:, :, 1:] - below[:, :, :-1]
-    counts_mine, counts_theirs = halves_of(counts, dp_id, 1)
-    query_mine, query_theirs = halves_of(queries[0], dp_id, 1)
-    new_mine, new_theirs = halves_of(new_kv[0], dp_id, 1)
-    counts_got, query_got, new_got = swapped((counts_theirs, query_theirs, new_theirs), "dp", 0)
-    all_counts = in_dp_order(counts_mine, counts_got, dp_id, 0)
-    query = in_dp_order(query_mine, query_got, dp_id, 0)
-    new_rows = jnp.transpose(in_dp_order(new_mine, new_got, dp_id, 0), (1, 0, 2))
-    is_here = (assign == ctx_id).astype(jnp.int32)
-    slot_counts = jnp.sum(all_counts * is_here[:, None, None], axis=0)
-    capacity = ctx_dev // 2
+    counts = jnp.transpose(counts.reshape(groups, 2, heads, ctx_count), (1, 0, 2, 3))
     offsets = jnp.arange(capacity, dtype=jnp.int32)
-    bias = jnp.where(offsets < slot_counts[:, :, None], 0.0, neg_large).astype(jnp.float32)
-    bias = bias.reshape(bias.shape[0], 1, ctx_count * capacity)
-    return order, query, new_rows, bias
-
-
-def local(cache, kept, assign, queries, new_kv, out_weight):
-    groups, kv_here, ctx_dev, width = cache.shape
-    if kv_here % 2 or lax.axis_size("ctx") != 8 or lax.axis_size("tensor") != 2:
-        return local_by_rows(cache, kept, assign, queries, new_kv, out_weight)
-    ctx_id = lax.axis_index("ctx")
-    capacity = ctx_dev // 2
-    per_group = queries.shape[2] // (kv_here * (width // 2))
-    order, query, new_rows, bias = prepare(cache, kept, assign, queries, new_kv)
+    bias = jnp.where(offsets < counts[..., None], 0.0, neg_large).astype(jnp.float32)
+    bias = bias.reshape(2, groups, heads, ctx_count * capacity)
+    new_sides = jnp.transpose(new_kv[0], (1, 0, 2)).reshape(2, heads, rows, width)
     places = places_of(
         kept.reshape(groups * kv_here, kept.shape[2]), ctx_id * ctx_dev, capacity
     )
     flat_cache = cache.reshape(groups * kv_here, ctx_dev, width)
-    received = relayout(flat_cache, places, order, groups)
-    head_out = attend_heads(query, received, bias, new_rows, per_group)
+    head_out = relayout_attend(flat_cache, places, order, groups, queries[0], new_sides, bias)
     return gather_project(head_out, out_weight, assign)
 
 

time: 146 us -> 133 us (0.911)
  Pallas kernels: 132 us -> 122 us
  starting transfers between devices: 5.13 us -> 0 us
  local copies, waits for them, and re-layouts: 5.59 us -> 7.43 us
    pallas_call x1, Pallas kernels: 63.1 us -> 54.2 us  [gather_project(): pl.pallas_call(gather_project_kernel, out_shape=jax.ShapeDtypeStruct((kep...]
    ppermute x3 -> x0, starting transfers between devices: 5.13 us -> none  [swapped(): lax.ppermute(array, axis, [(i, i ^ 1 << distance) for i in range(lax.axis...]
    unnamed x7 -> x11, local copies, waits for them, and re-layouts: 1.53 us -> 4.75 us
    dynamic_slice x6 -> x0, local copies, waits for them, and re-layouts: 2.38 us -> none  [the longest x5 2.37 us: halves_of(): mine = lax.dynamic_slice_in_dim(array, dp_id * size, size, axis)]
    pallas_call x2 -> x1, Pallas kernels: 66 us -> 65.3 us  [relayout_attend(): pl.pallas_call(relayout_kernel, out_shape=jax.ShapeDtypeStruct((2 * rows,...]
  transfers between devices with their start and end apart: 3 -> 0, of which waited for: 0 -> 0; matrix products, arithmetic and copies ran while one was open for 4% -> 0% of each run, Pallas kernels for 40% -> 0%
where the time goes in v4:
time: 133 us; the launch traced here: 132 us
  Pallas kernels  122 us (92%)
  local copies, waits for them, and re-layouts  7.43 us (6%)
  other arithmetic  2.45 us (2%)
    pallas_call x1, Pallas kernels, relayout_attend(): pl.pallas_call(relayout_kernel, out_shape=jax.ShapeDtypeStruct((2 * rows,...  65.3 us
    pallas_call x1, Pallas kernels, gather_project(): pl.pallas_call(gather_project_kernel, out_shape=jax.ShapeDtypeStruct((kep...  54.2 us
    unnamed x11, local copies, waits for them, and re-layouts  4.75 us
    pallas_call x1, Pallas kernels, places_of(): pl.pallas_call(places_kernel, out_shape=jax.ShapeDtypeStruct((kept_lists....  2.88 us

profile of v4, /device:TPU:0, one launch (start us, length us, event | category | flops | bytes accessed | tf_op | source)
XLA Modules:
  0.0 132.3 jit_solution(1305433139097392978)
XLA Ops:
  0.0 0.8 select_reduce_fusion.order_ref
  0.8 1.6 %convert_reduce_fusion = s32[4,4,9]{1,2,0:T(8,128)S(1)} fusion(s32[4,4,1024]{2,1,0:T(4,128)} %param.7, s32[9]{0:T(128)S(1)} %iota_multiply_fusion), kind=kLoop, calls=%fused_computation | loop fusion | flops 442224 | bytes 66148 | tf_op jit(solution)/shard_map/reduce_sum | solution.py:650
  2.4 0.1 copy.10
  2.5 1.5 %reshape.26.kept_ref = s32[16,1024]{1,0:T(8,128)} reshape(s32[4,4,1024]{2,1,0:T(4,128)} %param.7) | data formatting | bytes 131072 | tf_op jit(solution)/shard_map/reshape | solution.py:658
  4.0 2.9 %shard_map.64.places_ref = s32[16,1,256]{2,1,0:T(1,128)} custom-call(s32[1]{0:T(128)} %bitcast.start_ref, s32[16,1024]{1,0:T(8,128)} %reshape.26.kept_ref), custom_call_target="tpu_custom_call" | custom-call | tf_op jit(solution)/shard_map/pallas_call | solution.py:179
  6.9 0.1 lt.39
  7.0 0.1 lt.40
  7.1 0.1 compare_select_fusion.bias_hbm
  7.2 0.9 copy.9
  8.1 0.0 copy-start
  8.1 0.7 copy-done
  8.8 0.0 copy-start.2
  8.8 2.2 %copy-done.2 = bf16[4,4,512,256]{3,2,1,0:T(8,128)(2,1)S(1)} copy-done((bf16[4,4,512,256]{3,2,1,0:T(8,128)(2,1)S(1)}, bf16[4,4,512,256]{3,2,1,0:T(8,128)(2,1)}, u32[]{:S(2)}) %copy-start.2) | copy-done | bytes 4194328
  11.0 0.0 copy-start.3
  11.0 1.0 copy-done.3
  12.0 0.0 copy-start.1
  12.0 65.3 %shard_map.65.heads_ref = bf16[128,2048]{1,0:T(8,128)(2,1)S(1)} custom-call(s32[8]{0:T(128)S(1)} %select_reduce_fusion.order_ref, s32[16,1,256]{2,1,0:T(1,128)S(1)} %copy-done, bf16[16,512,256]{2,1,0:T(8,128)(2,1)S(1)} %bitcast.16, bf16[64,4096]{1,0:T(8,128)(2,1)S(1)} %bitcast.17, bf16[2,2,64,256]{3,2,1,0:T(8,128)(2,1)S(1)} %bitcast.15, ...), custom_call_target="tpu_custom_call" | custom-call | flops 30000001024 | bytes 150000000 | tf_op jit(solution)/shard_map/pallas_call | solution.py:364
  77.3 0.0 copy-done.1
  77.3 54.2 %shard_map.66 = bf16[4,64,1024]{2,1,0:T(8,128)(2,1)S(1)} custom-call(s32[8]{0:T(128)S(1)} %copy-done.1, bf16[128,2048]{1,0:T(8,128)(2,1)S(1)} %shard_map.65.heads_ref, bf16[4096,1024]{1,0:T(8,128)(2,1)} %weight_hbm.1), custom_call_target="tpu_custom_call" | custom-call | tf_op jit(solution)/shard_map/pallas_call | solution.py:610
  131.5 0.8 copy.14
  (5 shorter events, 0.0 us)
Async XLA Ops:
  8.1 0.7 copy-start
  8.8 2.2 %copy-start.2 = (bf16[4,4,512,256]{3,2,1,0:T(8,128)(2,1)S(1)}, bf16[4,4,512,256]{3,2,1,0:T(8,128)(2,1)}, u32[]{:S(2)}) copy-start(bf16[4,4,512,256]{3,2,1,0:T(8,128)(2,1)} %param.6) | copy-start | bytes 12582916
  11.0 1.0 copy-start.3
  12.0 65.3 %copy-start.1 = (s32[8]{0:T(128)S(1)}, s32[8]{0:T(128)}, u32[]{:S(2)}) copy-start(s32[8]{0:T(128)} %assign_ref.1) | copy-start | bytes 100

commit v5 on v4

--- a/solution.py
+++ b/solution.py
@@ -165,26 +165,27 @@
 
 def places_kernel(start_ref, kept_ref, out_ref):
     start = start_ref[0]
-    lists, total = kept_ref.shape
+    groups, kv_here, total = kept_ref.shape
     capacity = out_ref.shape[2]
-    for i in range(lists):
-        kept = kept_ref[i : i + 1]
+    for i in range(groups * kv_here):
+        g, h = i // kv_here, i % kv_here
+        kept = kept_ref[g, h : h + 1]
         first = jnp.sum((kept < start).astype(jnp.int32))
         wide = jnp.broadcast_to(kept, (8, total))
         rolled = pltpu.roll(wide, lax.rem(total - first, total), 1)
         out_ref[i] = rolled[:1, :capacity] - start
 
 
-def places_of(kept_lists, block_start, capacity):
+def places_of(kept, block_start, capacity):
     return pl.pallas_call(
         places_kernel,
-        out_shape=jax.ShapeDtypeStruct((kept_lists.shape[0], 1, capacity), jnp.int32),
+        out_shape=jax.ShapeDtypeStruct((kept.shape[0] * kept.shape[1], 1, capacity), jnp.int32),
         in_specs=[
             pl.BlockSpec(memory_space=pltpu.SMEM),
             pl.BlockSpec(memory_space=pltpu.VMEM),
         ],
         out_specs=pl.BlockSpec(memory_space=pltpu.VMEM),
-    )(block_start.reshape(1), kept_lists)
+    )(block_start.reshape(1), kept)
 
 
 def relayout_kernel(
@@ -393,7 +394,7 @@
         + [pltpu.VMEM((2 * groups, piece, width), kind)] * (heads * pieces),
         cost_estimate=pl.CostEstimate(flops=int(3e10), bytes_accessed=int(1.5e8), transcendentals=0),
         compiler_params=pltpu.CompilerParams(
-            collective_id=0, has_side_effects=True, vmem_limit_bytes=48 * 1024 * 1024
+            collective_id=0, has_side_effects=True, vmem_limit_bytes=60 * 1024 * 1024
         ),
     )(order, places, flat_cache, queries, new_sides, bias_sides)
 
@@ -511,8 +512,33 @@
     arrived(0, partner_x)
     up(0, partner_x)
     down(0, partner_x)
+    slots = gat.shape[1]
+    depth = gat.shape[3]
+    tiles = part.shape[0]
+    near = z // 2 * (slots // 2)
+    far = slots // 2 - near
+
+    def multiply(n, first):
+        span = pl.ds(pl.multiple_of(n * tile, tile), tile)
+        some = pl.ds(first, slots // 2)
+        flat = (slots // 2 * rows, depth)
+        product = jnp.dot(
+            gat[0, some].reshape(flat), weight[:depth, span], preferred_element_type=jnp.float32
+        ) + jnp.dot(
+            gat[1, some].reshape(flat), weight[depth:, span], preferred_element_type=jnp.float32
+        )
+        part[n, some] = product.reshape(slots // 2, rows, tile)
+
     for k in range(1, zs):
-        for piece in (1, 0, 2, 3):
+        if k == zs - 1:
+            for piece in z_first:
+                for zo in range(2):
+                    arrived(piece, near + zo * 2 + 1 - x)
+            load_weight.wait()
+        for index, piece in enumerate((1, 0, 2, 3)):
+            if k == zs - 1:
+                for n in range(index * tiles // 4, (index + 1) * tiles // 4):
+                    multiply(n, near)
             for base in (c, partner_x) if piece in x_first else (c,):
                 @pl.when(z >= k)
                 def _():
@@ -529,13 +555,8 @@
                         copy(piece, base + 2 * k, 2).start()
 
     for piece in z_first:
-        for zo in range(zs):
-            arrived(piece, zo * 2 + 1 - x)
-    load_weight.wait()
-
-    slots = gat.shape[1]
-    depth = gat.shape[3]
-    tiles = part.shape[0]
+        for zo in range(2):
+            arrived(piece, far + zo * 2 + 1 - x)
 
     def exchange(n):
         return pltpu.make_async_remote_copy(
@@ -544,13 +565,7 @@
         )
 
     def tile_step(n, carry):
-        span = pl.ds(pl.multiple_of(n * tile, tile), tile)
-        product = jnp.dot(
-            gat[0].reshape(slots * rows, depth), weight[:depth, span], preferred_element_type=jnp.float32
-        ) + jnp.dot(
-            gat[1].reshape(slots * rows, depth), weight[depth:, span], preferred_element_type=jnp.float32
-        )
-        part[n] = product.reshape(slots, rows, tile)
+        multiply(n, far)
         for j in range(kept):
             send_buf[n, j] = part[n, assign_ref[(1 - t) * kept + j]].astype(send_buf.dtype)
         exchange(n).start()
@@ -630,7 +645,7 @@
             dma,
         ],
         compiler_params=pltpu.CompilerParams(
-            collective_id=1, has_side_effects=True, vmem_limit_bytes=48 * 1024 * 1024
+            collective_id=1, has_side_effects=True, vmem_limit_bytes=60 * 1024 * 1024
         ),
     )(assign, head_out, out_weight)
 
@@ -654,9 +669,7 @@
     bias = jnp.where(offsets < counts[..., None], 0.0, neg_large).astype(jnp.float32)
     bias = bias.reshape(2, groups, heads, ctx_count * capacity)
     new_sides = jnp.transpose(new_kv[0], (1, 0, 2)).reshape(2, heads, rows, width)
-    places = places_of(
-        kept.reshape(groups * kv_here, kept.shape[2]), ctx_id * ctx_dev, capacity
-    )
+    places = places_of(kept, ctx_id * ctx_dev, capacity)
     flat_cache = cache.reshape(groups * kv_here, ctx_dev, width)
     head_out = relayout_attend(flat_cache, places, order, groups, queries[0], new_sides, bias)
     return gather_project(head_out, out_weight, assign)

time: 133 us -> 130 us (0.977)
  local copies, waits for them, and re-layouts: 7.43 us -> 3.73 us
    unnamed x11 -> x3, local copies, waits for them, and re-layouts: 4.75 us -> 1.88 us
    reshape x1 -> x0, local copies, waits for them, and re-layouts: 1.49 us -> none  [local(): kept.reshape(groups * kv_here, kept.shape[2])]
where the time goes in v5:
time: 130 us
  Pallas kernels  122 us (94%)
  local copies, waits for them, and re-layouts  3.73 us (3%)
  other arithmetic  3.66 us (3%)
    pallas_call x1, Pallas kernels, relayout_attend(): pl.pallas_call(relayout_kernel, out_shape=jax.ShapeDtypeStruct((2 * rows,...  66.3 us
    pallas_call x1, Pallas kernels, gather_project(): pl.pallas_call(gather_project_kernel, out_shape=jax.ShapeDtypeStruct((kep...  53.3 us
    pallas_call x1, Pallas kernels, places_of(): pl.pallas_call(places_kernel, out_shape=jax.ShapeDtypeStruct((kept.shape[...  2.88 us

profile of v5, /device:TPU:0, one launch (start us, length us, event | category | flops | bytes accessed | tf_op | source)
XLA Modules:
  0.0 129.9 jit_solution(15896944856812345005)
XLA Ops:
  0.0 1.3 %select_reduce_fusion.order_ref = s32[8]{0:T(128)} fusion(s32[8]{0:T(128)} %assign_ref.1), kind=kLoop, calls=%fused_computation.4 | loop fusion | flops 184 | bytes 64 | tf_op jit(solution)/shard_map/reduce_sum | solution.py:663
  1.4 2.9 %shard_map.64.places_ref = s32[16,1,256]{2,1,0:T(1,128)} custom-call(s32[1]{0:T(128)} %bitcast.start_ref, s32[4,4,1024]{2,1,0:T(4,128)} %kept_ref.1), custom_call_target="tpu_custom_call" | custom-call | tf_op jit(solution)/shard_map/pallas_call | solution.py:180
  4.2 1.6 %convert_reduce_fusion = s32[4,4,9]{1,2,0:T(8,128)S(1)} fusion(s32[4,4,1024]{2,1,0:T(4,128)} %kept_ref.1, s32[9]{0:T(128)S(1)} %iota_multiply_fusion), kind=kLoop, calls=%fused_computation | loop fusion | flops 442224 | bytes 66148 | tf_op jit(solution)/shard_map/reduce_sum | solution.py:665
  5.9 0.1 copy.10
  6.0 0.1 lt.39
  6.0 0.1 lt.40
  6.1 0.7 compare_select_fusion.bias_hbm
  6.9 1.6 %copy.9 = bf16[4,64,256]{2,1,0:T(8,128)(2,1)} copy(bf16[4,64,256]{2,0,1:T(4,128)(2,1)} %bitcast.15) | data formatting | bytes 262144 | tf_op jit(solution)/shard_map/transpose | solution.py:671
  8.4 66.3 %shard_map.65.heads_ref = bf16[128,2048]{1,0:T(8,128)(2,1)} custom-call(s32[8]{0:T(128)} %select_reduce_fusion.order_ref, s32[16,1,256]{2,1,0:T(1,128)} %shard_map.64.places_ref, bf16[16,512,256]{2,1,0:T(8,128)(2,1)} %bitcast.19, bf16[64,4096]{1,0:T(8,128)(2,1)} %bitcast.20, bf16[2,2,64,256]{3,2,1,0:T(8,128)(2,1)} %bitcast.16, ...), custom_call_target="tpu_custom_call" | custom-call | flops 30000001024 | bytes 150000000 | tf_op jit(solution)/shard_map/pallas_call | solution.py:365
  74.7 53.3 %shard_map.66 = bf16[4,64,1024]{2,1,0:T(8,128)(2,1)} custom-call(s32[8]{0:T(128)} %assign_ref.1, bf16[128,2048]{1,0:T(8,128)(2,1)} %shard_map.65.heads_ref, bf16[4096,1024]{1,0:T(8,128)(2,1)} %weight_hbm.1), custom_call_target="tpu_custom_call" | custom-call | tf_op jit(solution)/shard_map/pallas_call | solution.py:625
  128.0 1.9 %copy.14 = bf16[4,64,1024]{2,1,0:T(8,128)(2,1)} copy(bf16[4,64,1024]{2,1,0:T(8,128)(2,1)} %shard_map.66) | data formatting | bytes 1048576
  (5 shorter events, 0.0 us)

commit v6 on v5

--- a/solution.py
+++ b/solution.py
@@ -645,7 +645,7 @@
             dma,
         ],
         compiler_params=pltpu.CompilerParams(
-            collective_id=1, has_side_effects=True, vmem_limit_bytes=60 * 1024 * 1024
+            collective_id=1, has_side_effects=True, vmem_limit_bytes=48 * 1024 * 1024
         ),
     )(assign, head_out, out_weight)
 

time: 130 us -> 129 us (level)
    pallas_call x1, Pallas kernels: 53.3 us -> 51.9 us  [gather_project(): pl.pallas_call(gather_project_kernel, out_shape=jax.ShapeDtypeStruct((kep...]
where the time goes in v6:
time: 129 us
  Pallas kernels  121 us (94%)
  local copies, waits for them, and re-layouts  3.69 us (3%)
  other arithmetic  3.66 us (3%)
    pallas_call x1, Pallas kernels, relayout_attend(): pl.pallas_call(relayout_kernel, out_shape=jax.ShapeDtypeStruct((2 * rows,...  66.3 us
    pallas_call x1, Pallas kernels, gather_project(): pl.pallas_call(gather_project_kernel, out_shape=jax.ShapeDtypeStruct((kep...  51.9 us
    pallas_call x1, Pallas kernels, places_of(): pl.pallas_call(places_kernel, out_shape=jax.ShapeDtypeStruct((kept.shape[...  2.88 us

profile of v6, /device:TPU:0, one launch (start us, length us, event | category | flops | bytes accessed | tf_op | source)
XLA Modules:
  0.0 128.5 jit_solution(10338760645739882485)
XLA Ops:
  0.0 1.3 %select_reduce_fusion.order_ref = s32[8]{0:T(128)} fusion(s32[8]{0:T(128)} %assign_ref.1), kind=kLoop, calls=%fused_computation.4 | loop fusion | flops 184 | bytes 64 | tf_op jit(solution)/shard_map/reduce_sum | solution.py:663
  1.4 2.9 %shard_map.64.places_ref = s32[16,1,256]{2,1,0:T(1,128)} custom-call(s32[1]{0:T(128)} %bitcast.start_ref, s32[4,4,1024]{2,1,0:T(4,128)} %kept_ref.1), custom_call_target="tpu_custom_call" | custom-call | tf_op jit(solution)/shard_map/pallas_call | solution.py:180
  4.2 1.6 %convert_reduce_fusion = s32[4,4,9]{1,2,0:T(8,128)S(1)} fusion(s32[4,4,1024]{2,1,0:T(4,128)} %kept_ref.1, s32[9]{0:T(128)S(1)} %iota_multiply_fusion), kind=kLoop, calls=%fused_computation | loop fusion | flops 442224 | bytes 66148 | tf_op jit(solution)/shard_map/reduce_sum | solution.py:665
  5.9 0.1 copy.10
  6.0 0.1 lt.39
  6.0 0.1 lt.40
  6.1 0.7 compare_select_fusion.bias_hbm
  6.9 1.6 %copy.9 = bf16[4,64,256]{2,1,0:T(8,128)(2,1)} copy(bf16[4,64,256]{2,0,1:T(4,128)(2,1)} %bitcast.15) | data formatting | bytes 262144 | tf_op jit(solution)/shard_map/transpose | solution.py:671
  8.4 0.0 copy-start.1
  8.4 66.3 %shard_map.65.heads_ref = bf16[128,2048]{1,0:T(8,128)(2,1)} custom-call(s32[8]{0:T(128)} %select_reduce_fusion.order_ref, s32[16,1,256]{2,1,0:T(1,128)} %shard_map.64.places_ref, bf16[16,512,256]{2,1,0:T(8,128)(2,1)} %bitcast.19, bf16[64,4096]{1,0:T(8,128)(2,1)} %bitcast.20, bf16[2,2,64,256]{3,2,1,0:T(8,128)(2,1)} %bitcast.16, ...), custom_call_target="tpu_custom_call" | custom-call | flops 30000001024 | bytes 150000000 | tf_op jit(solution)/shard_map/pallas_call | solution.py:365
  74.7 0.0 copy-done.1
  74.8 0.0 copy-start
  74.8 1.0 copy-done
  75.8 51.9 %shard_map.66 = bf16[4,64,1024]{2,1,0:T(8,128)(2,1)S(1)} custom-call(s32[8]{0:T(128)S(1)} %copy-done.1, bf16[128,2048]{1,0:T(8,128)(2,1)S(1)} %copy-done, bf16[4096,1024]{1,0:T(8,128)(2,1)} %weight_hbm.1), custom_call_target="tpu_custom_call" | custom-call | tf_op jit(solution)/shard_map/pallas_call | solution.py:625
  127.7 0.8 copy.14
  (5 shorter events, 0.0 us)
Async XLA Ops:
  8.4 66.3 %copy-start.1 = (s32[8]{0:T(128)S(1)}, s32[8]{0:T(128)}, u32[]{:S(2)}) copy-start(s32[8]{0:T(128)} %assign_ref.1) | copy-start | bytes 100
  74.8 1.0 copy-start
